TPU v7x, 768 devices: a whole 4x8x12 slice. The times are simulated.
768 devices in a mesh: sec: 16 (over y, core), grp: 48 (over x, z).
Axes of the slice: x: 4, y: 8, z: 12, core: 2. Of those that a mesh axis runs over, the one named last changes fastest.
Arguments:
- positions: float32 [3, 393216], P(None, ('sec', 'grp')), may hold values from -9 to 9, as said below
- velocities: float32 [3, 393216], P(None, ('sec', 'grp')), may hold values from -4 to 4
- masses: float32 [393216], P(('sec', 'grp')), may hold values from 0.004 to 0.04
- near_list: int32 [1536, 64], P(('sec', 'grp')), may hold values from 0 to 31, as said below
- near_count: int32 [1536], P(('sec', 'grp')), may hold values from 1 to 64, as said below
- far_list: int32 [1536, 32], P(('sec', 'grp')), may hold values from 0 to 1535
Outputs:
- positions_out: float32 [3, 393216], P(None, ('sec', 'grp'))
- velocities_out: float32 [3, 393216], P(None, ('sec', 'grp'))
- accel_out: float32 [3, 393216], P(None, ('sec', 'grp'))
Inputs may be any that keep to these rules, and one draw needn't show every extreme that they name: `positions`: within the range stated, particles of a block lie near one another and blocks of a group near their group. `near_list`: numbers within the group: the section index times 2 plus the block's place on its device. Slot 0 names the block itself. `near_count`: some block has all 64 slots used.
All inputs are finite; a program needn't handle non-finite values.
Results may differ from a plain program's by a relative error of at most 0.0001.
Values sent between devices are 32-bit elements; how exact they have to be, the bound alone decides.
No kernel may reach another device: no remote copies, remote signals or barrier semaphores. Data moves between devices by JAX's collectives and lax.ppermute only.
A program may use at most 32 MiB of HBM per device.

v0:
```python
import jax
import jax.numpy as jnp
from jax import lax
from jax.sharding import PartitionSpec as P

timestep = 0.05
softening = 0.25


def joined_along(blocks, dim):
    blocks = jnp.moveaxis(blocks, 0, dim)
    shape = blocks.shape
    return blocks.reshape(*shape[:dim], shape[dim] * shape[dim + 1], *shape[dim + 2 :])


def sent_to_all(value, axis):
    copies = jnp.broadcast_to(value, (lax.axis_size(axis), *value.shape))
    return lax.all_to_all(copies, axis, split_axis=0, concat_axis=0, tiled=True)


def gather_directly(value, axis, dim):
    return joined_along(sent_to_all(value, axis), dim)


def pair_accel(target, source):
    delta_x = source[0][:, None, :] - target[0][:, :, None]
    delta_y = source[1][:, None, :] - target[1][:, :, None]
    delta_z = source[2][:, None, :] - target[2][:, :, None]
    square = delta_x * delta_x + delta_y * delta_y + delta_z * delta_z + softening
    weight = source[3][:, None, :] / (square * jnp.sqrt(square))
    return jnp.stack(
        [
            jnp.sum(weight * delta_x, -1),
            jnp.sum(weight * delta_y, -1),
            jnp.sum(weight * delta_z, -1),
        ]
    )


def far_accel(target, moment):
    rel_x = target[0][:, None, :] - moment[1][:, :, None]
    rel_y = target[1][:, None, :] - moment[2][:, :, None]
    rel_z = target[2][:, None, :] - moment[3][:, :, None]
    square = rel_x * rel_x + rel_y * rel_y + rel_z * rel_z + softening
    inv_three = 1.0 / (square * jnp.sqrt(square))
    inv_five = inv_three / square
    inv_seven = inv_five / square
    quad_x = (
        moment[4][..., None] * rel_x + moment[7][..., None] * rel_y + moment[8][..., None] * rel_z
    )
    quad_y = (
        moment[7][..., None] * rel_x + moment[5][..., None] * rel_y + moment[9][..., None] * rel_z
    )
    quad_z = (
        moment[8][..., None] * rel_x + moment[9][..., None] * rel_y + moment[6][..., None] * rel_z
    )
    inner = rel_x * quad_x + rel_y * quad_y + rel_z * quad_z
    mass = moment[0][..., None]
    acc_x = jnp.sum(
        -mass * rel_x * inv_three - quad_x * inv_five + 2.5 * inner * rel_x * inv_seven, 1
    )
    acc_y = jnp.sum(
        -mass * rel_y * inv_three - quad_y * inv_five + 2.5 * inner * rel_y * inv_seven, 1
    )
    acc_z = jnp.sum(
        -mass * rel_z * inv_three - quad_z * inv_five + 2.5 * inner * rel_z * inv_seven, 1
    )
    return jnp.stack([acc_x, acc_y, acc_z])


def block_moments(blocks):
    weight = blocks[3]
    mass = jnp.sum(weight, -1)
    centre_x = jnp.sum(weight * blocks[0], -1) / mass
    centre_y = jnp.sum(weight * blocks[1], -1) / mass
    centre_z = jnp.sum(weight * blocks[2], -1) / mass
    off_x = blocks[0] - centre_x[:, None]
    off_y = blocks[1] - centre_y[:, None]
    off_z = blocks[2] - centre_z[:, None]
    radius = off_x * off_x + off_y * off_y + off_z * off_z
    return jnp.stack(
        [
            mass,
            centre_x,
            centre_y,
            centre_z,
            jnp.sum(weight * (3.0 * off_x * off_x - radius), -1),
            jnp.sum(weight * (3.0 * off_y * off_y - radius), -1),
            jnp.sum(weight * (3.0 * off_z * off_z - radius), -1),
            jnp.sum(3.0 * weight * off_x * off_y, -1),
            jnp.sum(3.0 * weight * off_x * off_z, -1),
            jnp.sum(3.0 * weight * off_y * off_z, -1),
        ]
    )


def accelerate(half, masses, near_list, near_count, far_list):
    local_blocks = near_list.shape[0]
    block_size = half.shape[1] // local_blocks
    own = jnp.concatenate([half, masses[None, :]], 0)
    own_blocks = own.reshape(4, local_blocks, block_size)
    local_moments = block_moments(own_blocks)
    across = gather_directly(local_moments, "grp", 1)
    moments = lax.all_gather(across, "sec", axis=1, tiled=True)
    far = far_accel(own_blocks[:3], moments[:, far_list])
    ghosts = lax.all_gather(own, "sec", axis=1, tiled=True)
    group_blocks = ghosts.reshape(4, -1, block_size)
    longest = jnp.max(near_count)

    def add_slot(slot, total):
        source = jnp.take(group_blocks, near_list[:, slot], axis=1)
        live = (slot < near_count).astype(jnp.float32)
        return total + pair_accel(own_blocks[:3], source) * live[None, :, None]

    direct = lax.fori_loop(
        0, longest, add_slot, jnp.zeros((3, local_blocks, block_size), jnp.float32)
    )
    direct = direct.reshape(3, local_blocks * block_size)
    return direct + far.reshape(3, local_blocks * block_size)


def on_device(positions, velocities, masses, near_list, near_count, far_list):
    current = positions
    speed = velocities
    accel = jnp.zeros_like(positions)
    for step in range(2):
        half = current + 0.5 * timestep * speed
        accel = accelerate(half, masses, near_list, near_count, far_list)
        speed = speed + timestep * accel
        current = half + 0.5 * timestep * speed
    return (current, speed, accel)


def solution(mesh):
    placed = (
        P(None, ("sec", "grp")),
        P(None, ("sec", "grp")),
        P(("sec", "grp")),
        P(("sec", "grp"), None),
        P(("sec", "grp")),
        P(("sec", "grp"), None),
    )
    return jax.shard_map(
        on_device,
        mesh=mesh,
        in_specs=placed,
        out_specs=(P(None, ("sec", "grp")), P(None, ("sec", "grp")), P(None, ("sec", "grp"))),
        check_vma=False,
    )
```

profile of v0, /device:TPU:1, one launch (start us, length us, event | category | flops | bytes accessed | tf_op | source)
XLA Modules:
  0.0 412.2 jit_solution(15989409440922558665)
XLA Ops:
  4.3 19.0 %all-to-all-start = ((f32[48,10,2]{1,2,0:T(2,128)}), f32[48,10,2]{1,2,0:T(2,128)S(1)}, u32[]{:S(2)}, u32[]{:S(2)}) async-start(f32[48,10,2]{1,2,0:T(2,128)} %broadcast_in_dim.19), calls=%async_computation | async-start | bytes 98304 | tf_op jit(solution)/shard_map/all_to_all | solution.py:18
  24.1 18.7 %all_gather.12 = f32[4,8192]{1,0:T(4,128)S(1)} all-gather(f32[4,512]{1,0:T(4,128)S(1)} %pad_maximum_fusion.1), channel_id=1, replica_groups=mesh['sec'=16,'grp'=48] {'sec'}, dimensions={1}, use_global_device_ids=true | all-gather | bytes 139264 | tf_op jit(solution)/shard_map/all_gather | solution.py:106
  43.5 152.3 %while.20 = (s32[]{:T(128)}, f32[3,2,256]{2,1,0:T(2,128)S(1)}, s32[]{:T(128)}, s32[2,64]{0,1:T(8,128)S(1)}, f32[4,32,256]{2,0,1:T(4,128)S(1)}, /*index=5*/f32[4,...) while((s32[]{:T(128)}, f32[3,2,256]{2,1,0:T(2,128)S(1)}, s32[]{:T(128)}, ...), condition=%wide.region_5.7_spmd, body=%wide.region_1.6_spmd.sunk | while | flops 2235925 | bytes 121043 | solution.py:115
  44.9 0.9 fusion.119
  47.3 0.9 fusion.119
  49.7 0.9 fusion.119
  52.0 0.9 fusion.119
  54.4 0.9 fusion.119
  56.8 0.9 fusion.119
  59.2 0.9 fusion.119
  61.5 0.9 fusion.119
  63.9 0.9 fusion.119
  66.3 0.9 fusion.119
  68.6 0.9 fusion.119
  71.0 0.9 fusion.119
  73.4 0.9 fusion.119
  75.7 0.9 fusion.119
  78.1 0.9 fusion.119
  80.5 0.9 fusion.119
  82.9 0.9 fusion.119
  85.2 0.9 fusion.119
  87.6 0.9 fusion.119
  90.0 0.9 fusion.119
  92.3 0.9 fusion.119
  94.7 0.9 fusion.119
  97.1 0.9 fusion.119
  99.4 0.9 fusion.119
  101.8 0.9 fusion.119
  104.2 0.9 fusion.119
  106.6 0.9 fusion.119
  108.9 0.9 fusion.119
  111.3 0.9 fusion.119
  113.7 0.9 fusion.119
  116.0 0.9 fusion.119
  118.4 0.9 fusion.119
  120.8 0.9 fusion.119
  123.1 0.9 fusion.119
  125.5 0.9 fusion.119
  127.9 0.9 fusion.119
  130.3 0.9 fusion.119
  132.6 0.9 fusion.119
  135.0 0.9 fusion.119
  137.4 0.9 fusion.119
  139.7 0.9 fusion.119
  142.1 0.9 fusion.119
  144.5 0.9 fusion.119
  146.8 0.9 fusion.119
  149.2 0.9 fusion.119
  151.6 0.9 fusion.119
  154.0 0.9 fusion.119
  156.3 0.9 fusion.119
  158.7 0.9 fusion.119
  161.1 0.9 fusion.119
  163.4 0.9 fusion.119
  165.8 0.9 fusion.119
  168.2 0.9 fusion.119
  170.5 0.9 fusion.119
  172.9 0.9 fusion.119
  175.3 0.9 fusion.119
  196.1 14.8 %all-gather = f32[16,96,10]{1,2,0:T(8,128)S(1)} all-gather(f32[1,96,10]{1,2,0:T(8,128)S(1)} %copy.95), channel_id=1, replica_groups=mesh['sec'=16,'grp'=48] {'sec'}, dimensions={0}, use_global_device_ids=true | all-gather | bytes 65280 | tf_op jit(solution)/shard_map/all_gather | solution.py:104
  213.2 16.1 %all_gather.14 = f32[4,8192]{1,0:T(4,128)S(1)} all-gather(f32[4,512]{1,0:T(4,128)S(1)} %pad_maximum_fusion), channel_id=1, replica_groups=mesh['sec'=16,'grp'=48] {'sec'}, dimensions={1}, use_global_device_ids=true | all-gather | bytes 139264 | tf_op jit(solution)/shard_map/all_gather | solution.py:106
  231.2 11.9 %all-to-all-start.1 = ((f32[48,10,2]{1,2,0:T(2,128)}), f32[48,10,2]{1,2,0:T(2,128)S(1)}, u32[]{:S(2)}, u32[]{:S(2)}) async-start(f32[48,10,2]{1,2,0:T(2,128)} %broadcast_in_dim.34), calls=%async_computation.1 | async-start | bytes 98304 | tf_op jit(solution)/shard_map/all_to_all | solution.py:18
  243.1 152.2 %while.21 = (s32[]{:T(128)}, f32[3,2,256]{2,1,0:T(2,128)S(1)}, s32[]{:T(128)}, s32[2,64]{0,1:T(8,128)S(1)}, f32[4,32,256]{2,0,1:T(4,128)S(1)}, /*index=5*/f32[4,...) while((s32[]{:T(128)}, f32[3,2,256]{2,1,0:T(2,128)S(1)}, s32[]{:T(128)}, ...), condition=%wide.region_23.25_spmd, body=%wide.region_19.24_spmd.sunk | while | flops 2235925 | bytes 121043 | solution.py:115
  395.5 14.8 %all-gather.1 = f32[16,96,10]{1,2,0:T(8,128)S(1)} all-gather(f32[1,96,10]{1,2,0:T(8,128)S(1)} %copy.110), channel_id=1, replica_groups=mesh['sec'=16,'grp'=48] {'sec'}, dimensions={0}, use_global_device_ids=true | all-gather | bytes 65280 | tf_op jit(solution)/shard_map/all_gather | solution.py:104
  (1571 shorter events, 172.6 us)
Async XLA Ops:
  4.3 19.0 %copy-start.2 = (f32[512]{0:T(512)S(1)}, f32[512]{0:T(512)}, u32[]{:S(2)}) copy-start(f32[512]{0:T(512)} %param.14) | copy-start | bytes 6148
  4.3 191.7 %all-to-all-start = ((f32[48,10,2]{1,2,0:T(2,128)}), f32[48,10,2]{1,2,0:T(2,128)S(1)}, u32[]{:S(2)}, u32[]{:S(2)}) async-start(f32[48,10,2]{1,2,0:T(2,128)} %broadcast_in_dim.19), calls=%async_computation | async-start | bytes 98304 | tf_op jit(solution)/shard_map/all_to_all | solution.py:18
  23.3 0.7 copy-start.3
  24.1 18.7 %copy-start.1 = (s32[2]{0:T(128)S(1)}, s32[2]{0:T(128)}, u32[]{:S(2)}) copy-start(s32[2]{0:T(128)} %param.16) | copy-start | bytes 28
  43.5 152.4 %copy-start.4 = (s32[2,32]{1,0:T(2,128)S(1)}, s32[2,32]{1,0:T(2,128)}, u32[]{:S(2)}) copy-start(s32[2,32]{1,0:T(2,128)} %param.17) | copy-start | bytes 772
  212.2 0.7 copy-start
  231.2 164.2 %all-to-all-start.1 = ((f32[48,10,2]{1,2,0:T(2,128)}), f32[48,10,2]{1,2,0:T(2,128)S(1)}, u32[]{:S(2)}, u32[]{:S(2)}) async-start(f32[48,10,2]{1,2,0:T(2,128)} %broadcast_in_dim.34), calls=%async_computation.1 | async-start | bytes 98304 | tf_op jit(solution)/shard_map/all_to_all | solution.py:18
where the time goes:
time: 414 us; the launch traced here: 412 us
  other arithmetic  137 us (33%)
  loops' own time  94.9 us (23%)
  local copies, waits for them, and re-layouts  84.1 us (20%)
  blocking collectives  64.5 us (16%)
  starting transfers between devices  30.9 us (7%)
    reduce_sum x128, other arithmetic, pair_accel(): jnp.sum(weight * delta_x, -1)  111 us
    another operation x2, loops' own time, accelerate(): lax.fori_loop(0, longest, add_slot, jnp.zeros((3, local_blocks, block_siz...  94.9 us
    gather x128, local copies, waits for them, and re-layouts, add_slot(): source = jnp.take(group_blocks, near_list[:, slot], axis=1)  73.1 us
    all_gather x2, blocking collectives, accelerate(): ghosts = lax.all_gather(own, 'sec', axis=1, tiled=True)  34.9 us
    all_to_all x2, starting transfers between devices, sent_to_all(): return lax.all_to_all(copies, axis, split_axis=0, concat_axis=0, tiled=True)  30.9 us
    all_gather x2, blocking collectives, accelerate(): moments = lax.all_gather(across, 'sec', axis=1, tiled=True)  29.6 us
    add x128, other arithmetic, add_slot(): return total + pair_accel(own_blocks[:3], source) * live[None, :, None]  10.4 us
    select_n x128, other arithmetic, add_slot(): source = jnp.take(group_blocks, near_list[:, slot], axis=1)  9.57 us
  transfers between devices with their start and end apart: 2, of which 0 were waited for; matrix products, arithmetic and copies ran while one was open for 51% of the time, Pallas kernels for 0%

commit v1 on v0

v1 whole, which is shorter than its diff:
```python
import jax
import jax.numpy as jnp
from jax import lax
from jax.experimental import pallas as pl
from jax.experimental.pallas import tpu as pltpu
from jax.sharding import PartitionSpec as P

timestep = 0.05
softening = 0.25
N_SEC = 16
N_GRP = 48
B = 256
W = 2 * B
KBLK = 2 * N_SEC
LIST = 64
FAR = 32
CHUNK = 1024
f32 = jnp.float32
bf16 = jnp.bfloat16
VMEM = pl.BlockSpec(memory_space=pltpu.VMEM)
SMEM = pl.BlockSpec(memory_space=pltpu.SMEM)
PARAMS = pltpu.CompilerParams(vmem_limit_bytes=40 * 1024 * 1024)


def shape(*dims):
    return jax.ShapeDtypeStruct(dims, f32)


def split3(value):
    first = value.astype(bf16).astype(f32)
    rest = value - first
    second = rest.astype(bf16).astype(f32)
    return first, second, rest - second


def opening(pos_ref, vel_ref, mass_ref, near_ref, count_ref, send_ref, own_ref, times_ref):
    half = pos_ref[...] + (0.5 * timestep) * vel_ref[...]
    own = jnp.concatenate([half, mass_ref[...]], 0)
    own_ref[...] = own
    for d in range(N_SEC):
        send_ref[d] = own
    block = lax.broadcasted_iota(jnp.int32, (KBLK, LIST), 0)
    slot = lax.broadcasted_iota(jnp.int32, (KBLK, LIST), 1)
    for b in range(2):
        hit = (near_ref[b : b + 1, :] == block) & (slot < count_ref[b])
        times = jnp.sum(jnp.where(hit, 1.0, 0.0).astype(f32), axis=1, keepdims=True)
        times_ref[b] = jnp.broadcast_to(times, (KBLK, 128))


def group_moments(ghost_ref, out_ref):
    section = lax.broadcasted_iota(jnp.int32, (N_SEC, 128), 0)
    lane = lax.broadcasted_iota(jnp.int32, (N_SEC, 128), 1)
    base = section // 4 * 32
    packed = jnp.zeros((N_SEC, 128), f32)
    whole = [ghost_ref[:, c, :] for c in range(4)]

    def total(v):
        return jnp.sum(v, axis=1, keepdims=True)

    for place in range(2):
        x, y, z, m = [w[:, B * place : B * place + B] for w in whole]
        mass = total(m)
        centre = [total(m * v) / mass for v in (x, y, z)]
        dx, dy, dz = [v - c for v, c in zip((x, y, z), centre)]
        radius = dx * dx + dy * dy + dz * dz
        m3 = 3.0 * m
        numbers = [
            mass,
            *centre,
            total(m * (3.0 * dx * dx - radius)),
            total(m * (3.0 * dy * dy - radius)),
            total(m * (3.0 * dz * dz - radius)),
            total(m3 * dx * dy),
            total(m3 * dx * dz),
            total(m3 * dy * dz),
        ]
        for c, number in enumerate(numbers):
            packed = jnp.where(lane == base + (16 * place + c), number, packed)
    message = packed[0:4] + packed[4:8] + packed[8:12] + packed[12:16]
    for k in range(N_GRP):
        out_ref[k] = message


def direct(own_ref, ghost_ref, times_ref, out_ref, source_ref, weight_ref, total_ref):
    tot = ghost_ref[0]
    for d in range(1, N_SEC):
        tot = tot + ghost_ref[d]
    middle = jnp.sum(tot, axis=1, keepdims=True)[0:3] * (1.0 / (N_SEC * W))
    target = own_ref[0:3, :] - middle
    norm = jnp.sum(target * target, axis=0, keepdims=True) + softening
    pad = jnp.zeros((3, W), f32)
    a, b, c = split3(jnp.concatenate([-2.0 * target, jnp.ones((1, W), f32), norm, pad], 0))
    targets = jnp.concatenate([a, a, a, b, b, c], 0).astype(bf16)
    for d in range(N_SEC):
        ghost = ghost_ref[d]
        source = ghost[0:3] - middle
        mass = ghost[3:4]
        square = jnp.sum(source * source, axis=0, keepdims=True)
        a, b, c = split3(jnp.concatenate([source, square, jnp.ones((1, W), f32), pad], 0))
        source_ref[:, W * d : W * d + W] = jnp.concatenate([a, b, c, a, b, a], 0).astype(bf16)
        terms = jnp.concatenate([mass, source * mass], 0)
        both = []
        for t in range(2):
            first, second = times_ref[t, 2 * d : 2 * d + 1, :], times_ref[t, 2 * d + 1 : 2 * d + 2, :]
            both.append(terms * jnp.concatenate([first, first, second, second], 1))
        a, b, c = split3(jnp.concatenate(both, 0))
        weight_ref[:, W * d : W * d + W] = jnp.concatenate([a, b, c, jnp.zeros_like(a)], 0).astype(bf16)
    total_ref[...] = jnp.zeros_like(total_ref)

    @pl.loop(0, N_SEC * W // CHUNK, unroll=2)
    def _(step):
        at = pl.ds(pl.multiple_of(step * CHUNK, CHUNK), CHUNK)
        square = lax.dot_general(
            source_ref[:, at], targets, (((0,), (0,)), ((), ())), preferred_element_type=f32
        )
        inverse = lax.rsqrt(square)
        cube = inverse * inverse * inverse
        high = cube.astype(bf16)
        low = (cube - high.astype(f32)).astype(bf16)
        weight = weight_ref[:, at]
        total_ref[...] += jnp.dot(weight, high, preferred_element_type=f32) + jnp.dot(
            weight, low, preferred_element_type=f32
        )

    sums = total_ref[0:8] + total_ref[8:16] + total_ref[16:24]
    lane = lax.broadcasted_iota(jnp.int32, (4, W), 1)
    sums = jnp.where(lane < B, sums[0:4], sums[4:8])
    out_ref[...] = sums[1:4] - target * sums[0:1]


def far_field(own_ref, moments_ref, far_ref, picked_ref):
    for b in range(2):
        for e in range(FAR):
            block = far_ref[b, e]
            device = block // 2
            place = block - device * 2
            section = device // N_GRP
            group = device - section * N_GRP
            high = section // 4
            row = group * 4 + (section - high * 4)
            shift = (128 - (high * 32 + place * 16)) % 128
            line = moments_ref[pl.ds(row, 1), :]
            picked_ref[b * FAR + e : b * FAR + e + 1, :] = pltpu.roll(line, shift, 1)
    out = []
    for b in range(2):
        picked = picked_ref[FAR * b : FAR * b + FAR, :]
        mass, cx, cy, cz, qxx, qyy, qzz, qxy, qxz, qyz = [picked[:, c : c + 1] for c in range(10)]
        x, y, z = [own_ref[c : c + 1, B * b : B * b + B] for c in range(3)]
        x, y, z = x - cx, y - cy, z - cz
        square = x * x + y * y + z * z + softening
        inverse = lax.rsqrt(square)
        two = inverse * inverse
        three = inverse * two
        five = three * two
        seven = five * two
        quad_x = qxx * x + qxy * y + qxz * z
        quad_y = qxy * x + qyy * y + qyz * z
        quad_z = qxz * x + qyz * y + qzz * z
        along = 2.5 * (x * quad_x + y * quad_y + z * quad_z) * seven - mass * three
        out.append(
            jnp.concatenate(
                [
                    jnp.sum(along * r - quad * five, axis=0, keepdims=True)
                    for r, quad in ((x, quad_x), (y, quad_y), (z, quad_z))
                ],
                0,
            )
        )
    return jnp.concatenate(out, 1)


def first_step(own_ref, vel_ref, direct_ref, moments_ref, far_ref, send_ref, next_ref, speed_ref, picked_ref):
    accel = direct_ref[...] + far_field(own_ref, moments_ref, far_ref, picked_ref)
    speed = vel_ref[...] + timestep * accel
    speed_ref[...] = speed
    current = own_ref[0:3, :] + (0.5 * timestep) * speed
    half = current + (0.5 * timestep) * speed
    own = jnp.concatenate([half, own_ref[3:4, :]], 0)
    next_ref[...] = own
    for d in range(N_SEC):
        send_ref[d] = own


def last_step(own_ref, vel_ref, direct_ref, moments_ref, far_ref, pos_ref, speed_ref, accel_ref, picked_ref):
    accel = direct_ref[...] + far_field(own_ref, moments_ref, far_ref, picked_ref)
    accel_ref[...] = accel
    speed = vel_ref[...] + timestep * accel
    speed_ref[...] = speed
    pos_ref[...] = own_ref[0:3, :] + (0.5 * timestep) * speed


def on_device(positions, velocities, masses, near_list, near_count, far_list):
    send, own, times = pl.pallas_call(
        opening,
        out_shape=(shape(N_SEC, 4, W), shape(4, W), shape(2, KBLK, 128)),
        in_specs=[VMEM, VMEM, VMEM, VMEM, SMEM],
        out_specs=(VMEM, VMEM, VMEM),
        compiler_params=PARAMS,
    )(positions, velocities, masses.reshape(1, W), near_list, near_count)
    speed = velocities
    for step in range(2):
        ghosts = lax.all_to_all(send, "sec", split_axis=0, concat_axis=0, tiled=True)
        message = pl.pallas_call(
            group_moments,
            out_shape=shape(N_GRP, 4, 128),
            in_specs=[VMEM],
            out_specs=VMEM,
            compiler_params=PARAMS,
        )(ghosts)
        moments = lax.all_to_all(message, "grp", split_axis=0, concat_axis=0, tiled=True)
        near = pl.pallas_call(
            direct,
            out_shape=shape(3, W),
            in_specs=[VMEM] * 3,
            out_specs=VMEM,
            scratch_shapes=[
                pltpu.VMEM((48, N_SEC * W), bf16),
                pltpu.VMEM((32, N_SEC * W), bf16),
                pltpu.VMEM((32, W), f32),
            ],
            compiler_params=PARAMS,
            cost_estimate=pl.CostEstimate(
                flops=2 * 80 * W * N_SEC * W, bytes_accessed=200000, transcendentals=W * N_SEC * W
            ),
        )(own, ghosts, times)
        last = step == 1
        made = pl.pallas_call(
            last_step if last else first_step,
            out_shape=(shape(3, W),) * 3 if last else (shape(N_SEC, 4, W), shape(4, W), shape(3, W)),
            in_specs=[VMEM, VMEM, VMEM, VMEM, SMEM],
            out_specs=(VMEM,) * 3,
            scratch_shapes=[pltpu.VMEM((2 * FAR, 128), f32)],
            compiler_params=PARAMS,
        )(own, speed, near, moments.reshape(N_GRP * 4, 128), far_list)
        if last:
            return made
        send, own, speed = made


def solution(mesh):
    placed = (
        P(None, ("sec", "grp")),
        P(None, ("sec", "grp")),
        P(("sec", "grp")),
        P(("sec", "grp"), None),
        P(("sec", "grp")),
        P(("sec", "grp"), None),
    )
    return jax.shard_map(
        on_device,
        mesh=mesh,
        in_specs=placed,
        out_specs=(P(None, ("sec", "grp")), P(None, ("sec", "grp")), P(None, ("sec", "grp"))),
        check_vma=False,
    )
```

time: 414 us -> 91 us (0.22)
  other arithmetic: 137 us -> 0 us
  loops' own time: 94.9 us -> 0 us
  local copies, waits for them, and re-layouts: 84.1 us -> 2.77 us
  blocking collectives: 64.5 us -> 35.4 us
  Pallas kernels: 0 us -> 21.5 us
  starting transfers between devices: 30.9 us -> 19.6 us
  waiting for transfers between devices: 0.01 us -> 10.6 us
    reduce_sum x134 -> x0, other arithmetic: 112 us -> none  [the longest x128 111 us: pair_accel(): jnp.sum(weight * delta_x, -1)]
    another operation x2 -> x0, loops' own time: 94.9 us -> none  [accelerate(): lax.fori_loop(0, longest, add_slot, jnp.zeros((3, local_blocks, block_siz...]
    gather x132 -> x0, local copies, waits for them, and re-layouts: 74.5 us -> none  [the longest x128 73.1 us: add_slot(): source = jnp.take(group_blocks, near_list[:, slot], axis=1)]
    all_gather x4 -> x0, blocking collectives: 64.5 us -> none  [the longest x2 34.9 us: accelerate(): ghosts = lax.all_gather(own, 'sec', axis=1, tiled=True)]
    all_to_all x0 -> x2, blocking collectives: none -> 35.4 us  [on_device(): lax.all_to_all(send, 'sec', split_axis=0, concat_axis=0, tiled=True)]
    pallas_call x0 -> x7, Pallas kernels: none -> 21.5 us  [the longest x2 14.4 us: on_device(): pl.pallas_call(direct, out_shape=shape(3, W), in_specs=[VMEM] * 3, out_sp...]
    add x131 -> x0, other arithmetic: 11.7 us -> none  [the longest x128 10.4 us: add_slot(): return total + pair_accel(own_blocks[:3], source) * live[None, :, None]]
    all_to_all x2, starting transfers between devices: 30.9 us -> 19.6 us  [on_device(): lax.all_to_all(message, 'grp', split_axis=0, concat_axis=0, tiled=True)]
  transfers between devices with their start and end apart: 2 -> 2, of which waited for: 0 -> 2; matrix products, arithmetic and copies ran while one was open for 51% -> 0% of each run, Pallas kernels for 0% -> 16%
where the time goes in v1:
time: 91 us; the launch traced here: 90.5 us
  blocking collectives  35.4 us (39%)
  Pallas kernels  21.5 us (24%)
  starting transfers between devices  19.6 us (22%)
  waiting for transfers between devices  10.6 us (12%)
  local copies, waits for them, and re-layouts  2.77 us (3%)
    all_to_all x2, blocking collectives, on_device(): lax.all_to_all(send, 'sec', split_axis=0, concat_axis=0, tiled=True)  35.4 us
    all_to_all x2, starting transfers between devices, on_device(): lax.all_to_all(message, 'grp', split_axis=0, concat_axis=0, tiled=True)  19.6 us
    pallas_call x2, Pallas kernels, on_device(): pl.pallas_call(direct, out_shape=shape(3, W), in_specs=[VMEM] * 3, out_sp...  14.4 us
    all_to_all x2, waiting for transfers between devices, on_device(): lax.all_to_all(message, 'grp', split_axis=0, concat_axis=0, tiled=True)  10.6 us
    pallas_call x2, Pallas kernels, on_device(): pl.pallas_call(last_step if last else first_step, out_shape=(shape(3, W),...  4.7 us
    unnamed x14, local copies, waits for them, and re-layouts  2.77 us
  transfers between devices with their start and end apart: 2, of which 2 were waited for; matrix products, arithmetic and copies ran while one was open for 0% of the time, Pallas kernels for 16%

profile of v1, /device:TPU:1, one launch (start us, length us, event | category | flops | bytes accessed | tf_op | source)
XLA Modules:
  0.0 90.5 jit_solution(14371665405871661135)
XLA Ops:
  0.6 0.0 copy-start.6
  0.6 0.0 copy-start.5
  0.7 0.6 copy-done.6
  1.3 0.0 copy-done.5
  1.3 0.0 copy-start
  1.3 0.7 copy-done
  2.0 0.0 copy-start.2
  2.0 0.7 copy-done.2
  2.7 0.0 copy-start.4
  2.7 0.7 copy-done.4
  3.4 0.6 shard_map.85
  4.0 22.1 %all_to_all.20.ghost_ref = f32[16,4,512]{2,1,0:T(4,128)S(1)} all-to-all(f32[16,4,512]{2,1,0:T(4,128)S(1)} %get-tuple-element.10), channel_id=1, replica_groups=mesh['sec'=16,'grp'=48] {'sec'}, dimensions={0} | all-to-all | bytes 262144 | tf_op jit(solution)/shard_map/all_to_all | solution.py:202
  26.2 0.9 shard_map.87
  27.0 13.5 %all-to-all-start.1 = ((f32[48,4,128]{2,1,0:T(4,128)}), f32[48,4,128]{2,1,0:T(4,128)S(1)}, u32[]{:S(2)}, u32[]{:S(2)}) async-start(f32[48,4,128]{2,1,0:T(4,128)} %shard_map.87), calls=%async_computation.1 | async-start | bytes 196608 | tf_op jit(solution)/shard_map/all_to_all | solution.py:210
  40.5 0.0 copy-start.1
  40.5 7.2 %shard_map.86.direct_ref = f32[3,512]{1,0:T(4,128)S(1)} custom-call(f32[4,512]{1,0:T(4,128)S(1)} %get-tuple-element.9.own_ref, f32[16,4,512]{2,1,0:T(4,128)S(1)} %all_to_all.20.ghost_ref, f32[2,32,128]{2,1,0:T(8,128)S(1)} %get-tuple-element.11.times_ref), custom_call_target="tpu_custom_call" | custom-call | flops 671088640 | bytes 200000 | tf_op jit(solution)/shard_map/pallas_call | solution.py:211
  47.7 0.0 copy-start.3
  47.7 5.3 %all-to-all-done.1 = f32[48,4,128]{2,1,0:T(4,128)S(1)} async-done(((f32[48,4,128]{2,1,0:T(4,128)}), f32[48,4,128]{2,1,0:T(4,128)S(1)}, u32[]{:S(2)}, u32[]{:S(2)}) %all-to-all-start.1) | async-done | bytes 98336 | tf_op jit(solution)/shard_map/all_to_all | solution.py:210
  53.0 0.0 copy-done.1
  53.0 0.0 copy-done.3
  53.0 2.1 %shard_map.88 = (f32[16,4,512]{2,1,0:T(4,128)S(1)}, f32[4,512]{1,0:T(4,128)S(1)}, f32[3,512]{1,0:T(4,128)S(1)}) custom-call(f32[4,512]{1,0:T(4,128)S(1)} %get-tuple-element.9.own_ref, f32[3,512]{1,0:T(4,128)S(1)} %copy-done.1, f32[3,512]{1,0:T(4,128)S(1)} %shard_map.86.direct_ref, f32[192,128]{1,0:T(8,128)S(1)} %bitcast.4, s32[2,32]{1,0:T(2,128)S(1)} %copy-done.3), custom_call_target="tpu_custom_call" | custom-call | tf_op jit(solution)/shard_map/pallas_call | solution.py:227
  55.1 13.3 %all_to_all.21.ghost_ref = f32[16,4,512]{2,1,0:T(4,128)S(1)} all-to-all(f32[16,4,512]{2,1,0:T(4,128)S(1)} %get-tuple-element.14), channel_id=1, replica_groups=mesh['sec'=16,'grp'=48] {'sec'}, dimensions={0} | all-to-all | bytes 262144 | tf_op jit(solution)/shard_map/all_to_all | solution.py:202
  68.4 0.9 shard_map.90
  69.3 6.1 %all-to-all-start.3 = ((f32[48,4,128]{2,1,0:T(4,128)}), f32[48,4,128]{2,1,0:T(4,128)S(1)}, u32[]{:S(2)}, u32[]{:S(2)}) async-start(f32[48,4,128]{2,1,0:T(4,128)} %shard_map.90), calls=%async_computation.3 | async-start | bytes 196608 | tf_op jit(solution)/shard_map/all_to_all | solution.py:210
  75.4 7.2 %shard_map.89.direct_ref = f32[3,512]{1,0:T(4,128)S(1)} custom-call(f32[4,512]{1,0:T(4,128)S(1)} %get-tuple-element.12.own_ref, f32[16,4,512]{2,1,0:T(4,128)S(1)} %all_to_all.21.ghost_ref, f32[2,32,128]{2,1,0:T(8,128)S(1)} %get-tuple-element.11.times_ref), custom_call_target="tpu_custom_call" | custom-call | flops 671088640 | bytes 200000 | tf_op jit(solution)/shard_map/pallas_call | solution.py:211
  82.6 5.3 %all-to-all-done.3 = f32[48,4,128]{2,1,0:T(4,128)S(1)} async-done(((f32[48,4,128]{2,1,0:T(4,128)}), f32[48,4,128]{2,1,0:T(4,128)S(1)}, u32[]{:S(2)}, u32[]{:S(2)}) %all-to-all-start.3) | async-done | bytes 98336 | tf_op jit(solution)/shard_map/all_to_all | solution.py:210
  87.9 2.6 %shard_map.91 = (f32[3,512]{1,0:T(4,128)}, f32[3,512]{1,0:T(4,128)}, f32[3,512]{1,0:T(4,128)}) custom-call(f32[4,512]{1,0:T(4,128)S(1)} %get-tuple-element.12.own_ref, f32[3,512]{1,0:T(4,128)S(1)} %get-tuple-element.13.vel_ref, f32[3,512]{1,0:T(4,128)S(1)} %shard_map.89.direct_ref, f32[192,128]{1,0:T(8,128)S(1)} %bitcast.3, s32[2,32]{1,0:T(2,128)S(1)} %copy-done.3), custom_call_target="tpu_custom_call" | custom-call | tf_op jit(solution)/shard_map/pallas_call | solution.py:227
Async XLA Ops:
  0.6 0.7 copy-start.6
  0.6 0.7 copy-start.5
  1.3 0.7 copy-start
  2.0 0.7 copy-start.2
  2.7 0.7 copy-start.4
  27.0 26.0 %all-to-all-start.1 = ((f32[48,4,128]{2,1,0:T(4,128)}), f32[48,4,128]{2,1,0:T(4,128)S(1)}, u32[]{:S(2)}, u32[]{:S(2)}) async-start(f32[48,4,128]{2,1,0:T(4,128)} %shard_map.87), calls=%async_computation.1 | async-start | bytes 196608 | tf_op jit(solution)/shard_map/all_to_all | solution.py:210
  40.5 12.5 %copy-start.1 = (f32[3,512]{1,0:T(4,128)S(1)}, f32[3,512]{1,0:T(4,128)}, u32[]{:S(2)}) copy-start(f32[3,512]{1,0:T(4,128)} %vel_ref.3) | copy-start | bytes 18436
  47.7 5.3 %copy-start.3 = (s32[2,32]{1,0:T(2,128)S(1)}, s32[2,32]{1,0:T(2,128)}, u32[]{:S(2)}) copy-start(s32[2,32]{1,0:T(2,128)} %far_ref.3) | copy-start | bytes 772
  69.3 18.7 %all-to-all-start.3 = ((f32[48,4,128]{2,1,0:T(4,128)}), f32[48,4,128]{2,1,0:T(4,128)S(1)}, u32[]{:S(2)}, u32[]{:S(2)}) async-start(f32[48,4,128]{2,1,0:T(4,128)} %shard_map.90), calls=%async_computation.3 | async-start | bytes 196608 | tf_op jit(solution)/shard_map/all_to_all | solution.py:210

commit v2 on v1

--- a/solution.py
+++ b/solution.py
@@ -7,6 +7,7 @@
 
 timestep = 0.05
 softening = 0.25
+N_Y = 8
 N_SEC = 16
 N_GRP = 48
 B = 256
@@ -19,6 +20,7 @@
 bf16 = jnp.bfloat16
 VMEM = pl.BlockSpec(memory_space=pltpu.VMEM)
 SMEM = pl.BlockSpec(memory_space=pltpu.SMEM)
+WHOLE = pltpu.CompilerParams(vmem_limit_bytes=62 * 1024 * 1024)
 PARAMS = pltpu.CompilerParams(vmem_limit_bytes=40 * 1024 * 1024)
 
 
@@ -33,18 +35,20 @@
     return first, second, rest - second
 
 
-def opening(pos_ref, vel_ref, mass_ref, near_ref, count_ref, send_ref, own_ref, times_ref):
+def opening(pos_hbm, vel_hbm, mass_hbm, send_ref, own_ref, pos_ref, vel_ref, mass_ref, sems):
+    copies = [
+        pltpu.make_async_copy(source, target, sems.at[i])
+        for i, (source, target) in enumerate(((pos_hbm, pos_ref), (vel_hbm, vel_ref), (mass_hbm, mass_ref)))
+    ]
+    for copy in copies:
+        copy.start()
+    for copy in copies:
+        copy.wait()
     half = pos_ref[...] + (0.5 * timestep) * vel_ref[...]
     own = jnp.concatenate([half, mass_ref[...]], 0)
     own_ref[...] = own
-    for d in range(N_SEC):
+    for d in range(N_Y):
         send_ref[d] = own
-    block = lax.broadcasted_iota(jnp.int32, (KBLK, LIST), 0)
-    slot = lax.broadcasted_iota(jnp.int32, (KBLK, LIST), 1)
-    for b in range(2):
-        hit = (near_ref[b : b + 1, :] == block) & (slot < count_ref[b])
-        times = jnp.sum(jnp.where(hit, 1.0, 0.0).astype(f32), axis=1, keepdims=True)
-        times_ref[b] = jnp.broadcast_to(times, (KBLK, 128))
 
 
 def group_moments(ghost_ref, out_ref):
@@ -81,7 +85,13 @@
         out_ref[k] = message
 
 
-def direct(own_ref, ghost_ref, times_ref, out_ref, source_ref, weight_ref, total_ref):
+def direct(own_ref, ghost_ref, near_ref, count_ref, out_ref, source_ref, weight_ref, total_ref, times_ref):
+    block = lax.broadcasted_iota(jnp.int32, (KBLK, LIST), 0)
+    slot = lax.broadcasted_iota(jnp.int32, (KBLK, LIST), 1)
+    for b in range(2):
+        hit = (near_ref[b : b + 1, :] == block) & (slot < count_ref[b])
+        times = jnp.sum(jnp.where(hit, 1.0, 0.0).astype(f32), axis=1, keepdims=True)
+        times_ref[b] = jnp.broadcast_to(times, (KBLK, 128))
     tot = ghost_ref[0]
     for d in range(1, N_SEC):
         tot = tot + ghost_ref[d]
@@ -99,9 +109,10 @@
         a, b, c = split3(jnp.concatenate([source, square, jnp.ones((1, W), f32), pad], 0))
         source_ref[:, W * d : W * d + W] = jnp.concatenate([a, b, c, a, b, a], 0).astype(bf16)
         terms = jnp.concatenate([mass, source * mass], 0)
+        k = (d % N_Y * 2 + d // N_Y) * 2
         both = []
         for t in range(2):
-            first, second = times_ref[t, 2 * d : 2 * d + 1, :], times_ref[t, 2 * d + 1 : 2 * d + 2, :]
+            first, second = times_ref[t, k : k + 1, :], times_ref[t, k + 1 : k + 2, :]
             both.append(terms * jnp.concatenate([first, first, second, second], 1))
         a, b, c = split3(jnp.concatenate(both, 0))
         weight_ref[:, W * d : W * d + W] = jnp.concatenate([a, b, c, jnp.zeros_like(a)], 0).astype(bf16)
@@ -132,13 +143,12 @@
     for b in range(2):
         for e in range(FAR):
             block = far_ref[b, e]
-            device = block // 2
-            place = block - device * 2
-            section = device // N_GRP
+            device = block >> 1
+            section = (device * 1366) >> 16
             group = device - section * N_GRP
-            high = section // 4
-            row = group * 4 + (section - high * 4)
-            shift = (128 - (high * 32 + place * 16)) % 128
+            at = (section & 1) * N_Y + (section >> 1)
+            row = group * 4 + (at & 3)
+            shift = (128 - (at >> 2) * 32 - (block & 1) * 16) & 127
             line = moments_ref[pl.ds(row, 1), :]
             picked_ref[b * FAR + e : b * FAR + e + 1, :] = pltpu.roll(line, shift, 1)
     out = []
@@ -177,7 +187,7 @@
     half = current + (0.5 * timestep) * speed
     own = jnp.concatenate([half, own_ref[3:4, :]], 0)
     next_ref[...] = own
-    for d in range(N_SEC):
+    for d in range(N_Y):
         send_ref[d] = own
 
 
@@ -190,16 +200,23 @@
 
 
 def on_device(positions, velocities, masses, near_list, near_count, far_list):
-    send, own, times = pl.pallas_call(
+    send, own = pl.pallas_call(
         opening,
-        out_shape=(shape(N_SEC, 4, W), shape(4, W), shape(2, KBLK, 128)),
-        in_specs=[VMEM, VMEM, VMEM, VMEM, SMEM],
-        out_specs=(VMEM, VMEM, VMEM),
-        compiler_params=PARAMS,
-    )(positions, velocities, masses.reshape(1, W), near_list, near_count)
+        out_shape=(shape(N_Y, 4, W), shape(4, W)),
+        in_specs=[pl.BlockSpec(memory_space=pl.ANY)] * 3,
+        out_specs=(VMEM, VMEM),
+        scratch_shapes=[
+            pltpu.VMEM((3, W), f32),
+            pltpu.VMEM((3, W), f32),
+            pltpu.VMEM((1, W), f32),
+            pltpu.SemaphoreType.DMA((3,)),
+        ],
+        compiler_params=WHOLE,
+    )(positions, velocities, masses.reshape(1, W))
     speed = velocities
     for step in range(2):
-        ghosts = lax.all_to_all(send, "sec", split_axis=0, concat_axis=0, tiled=True)
+        along = lax.all_to_all(send, "y", split_axis=0, concat_axis=0, tiled=True)
+        ghosts = lax.all_gather(along, "core", axis=0, tiled=True)
         message = pl.pallas_call(
             group_moments,
             out_shape=shape(N_GRP, 4, 128),
@@ -211,22 +228,23 @@
         near = pl.pallas_call(
             direct,
             out_shape=shape(3, W),
-            in_specs=[VMEM] * 3,
+            in_specs=[VMEM, VMEM, VMEM, SMEM],
             out_specs=VMEM,
             scratch_shapes=[
                 pltpu.VMEM((48, N_SEC * W), bf16),
                 pltpu.VMEM((32, N_SEC * W), bf16),
                 pltpu.VMEM((32, W), f32),
+                pltpu.VMEM((2, KBLK, 128), f32),
             ],
             compiler_params=PARAMS,
             cost_estimate=pl.CostEstimate(
                 flops=2 * 80 * W * N_SEC * W, bytes_accessed=200000, transcendentals=W * N_SEC * W
             ),
-        )(own, ghosts, times)
+        )(own, ghosts, near_list, near_count)
         last = step == 1
         made = pl.pallas_call(
             last_step if last else first_step,
-            out_shape=(shape(3, W),) * 3 if last else (shape(N_SEC, 4, W), shape(4, W), shape(3, W)),
+            out_shape=(shape(3, W),) * 3 if last else (shape(N_Y, 4, W), shape(4, W), shape(3, W)),
             in_specs=[VMEM, VMEM, VMEM, VMEM, SMEM],
             out_specs=(VMEM,) * 3,
             scratch_shapes=[pltpu.VMEM((2 * FAR, 128), f32)],
@@ -238,18 +256,13 @@
 
 
 def solution(mesh):
-    placed = (
-        P(None, ("sec", "grp")),
-        P(None, ("sec", "grp")),
-        P(("sec", "grp")),
-        P(("sec", "grp"), None),
-        P(("sec", "grp")),
-        P(("sec", "grp"), None),
-    )
+    parts = jax.sharding.Mesh(mesh.devices.reshape(N_Y, 2, N_GRP), ("y", "core", "grp"))
+    every = ("y", "core", "grp")
+    placed = (P(None, every), P(None, every), P(every), P(every, None), P(every), P(every, None))
     return jax.shard_map(
         on_device,
-        mesh=mesh,
+        mesh=parts,
         in_specs=placed,
-        out_specs=(P(None, ("sec", "grp")), P(None, ("sec", "grp")), P(None, ("sec", "grp"))),
+        out_specs=(P(None, every),) * 3,
         check_vma=False,
     )

time: 91 us -> 90 us (0.989)
  waiting for transfers between devices: 10.6 us -> 7.58 us
  blocking collectives: 35.4 us -> 38.3 us
  local copies, waits for them, and re-layouts: 2.77 us -> 0.67 us
  starting transfers between devices: 19.6 us -> 20.7 us
    all_gather x0 -> x2, blocking collectives: none -> 13.8 us  [on_device(): ghosts = lax.all_gather(along, 'core', axis=0, tiled=True)]
    all_to_all x2, blocking collectives: 35.4 us -> 24.5 us  [on_device(): along = lax.all_to_all(send, 'y', split_axis=0, concat_axis=0, tiled=True)]
    all_to_all x2, waiting for transfers between devices: 10.6 us -> 7.58 us  [on_device(): lax.all_to_all(message, 'grp', split_axis=0, concat_axis=0, tiled=True)]
    unnamed x14 -> x10, local copies, waits for them, and re-layouts: 2.77 us -> 0.67 us
    pallas_call x3, Pallas kernels: 15 us -> 16.8 us  [the longest x2 15.5 us: on_device(): pl.pallas_call(direct, out_shape=shape(3, W), in_specs=[VMEM, VMEM, VMEM,...]
    pallas_call x2, Pallas kernels: 4.7 us -> 2.95 us  [on_device(): pl.pallas_call(last_step if last else first_step, out_shape=(shape(3, W),...]
    all_to_all x2, starting transfers between devices: 19.6 us -> 20.7 us  [on_device(): lax.all_to_all(message, 'grp', split_axis=0, concat_axis=0, tiled=True)]
  transfers between devices with their start and end apart: 2 -> 2, of which waited for: 2 -> 2; matrix products, arithmetic and copies ran while one was open for 0% -> 0% of each run, Pallas kernels for 16% -> 17%
where the time goes in v2:
time: 90 us; the launch traced here: 89.5 us
  blocking collectives  38.3 us (43%)
  Pallas kernels  21.6 us (24%)
  starting transfers between devices  20.7 us (23%)
  waiting for transfers between devices  7.58 us (8%)
    all_to_all x2, blocking collectives, on_device(): along = lax.all_to_all(send, 'y', split_axis=0, concat_axis=0, tiled=True)  24.5 us
    all_to_all x2, starting transfers between devices, on_device(): lax.all_to_all(message, 'grp', split_axis=0, concat_axis=0, tiled=True)  20.7 us
    pallas_call x2, Pallas kernels, on_device(): pl.pallas_call(direct, out_shape=shape(3, W), in_specs=[VMEM, VMEM, VMEM,...  15.5 us
    all_gather x2, blocking collectives, on_device(): ghosts = lax.all_gather(along, 'core', axis=0, tiled=True)  13.8 us
    all_to_all x2, waiting for transfers between devices, on_device(): lax.all_to_all(message, 'grp', split_axis=0, concat_axis=0, tiled=True)  7.58 us
    pallas_call x2, Pallas kernels, on_device(): pl.pallas_call(last_step if last else first_step, out_shape=(shape(3, W),...  2.95 us
  transfers between devices with their start and end apart: 2, of which 2 were waited for; matrix products, arithmetic and copies ran while one was open for 0% of the time, Pallas kernels for 17%

profile of v2, /device:TPU:1, one launch (start us, length us, event | category | flops | bytes accessed | tf_op | source)
XLA Modules:
  0.0 89.5 jit_solution(9139843182450518800)
XLA Ops:
  0.6 1.4 %shard_map.85 = (f32[8,4,512]{2,1,0:T(4,128)}, f32[4,512]{1,0:T(4,128)}) custom-call(f32[3,512]{1,0:T(4,128)} %pos_hbm.1, f32[3,512]{1,0:T(4,128)} %vel_ref.1, f32[1,512]{1,0:T(1,128)} %bitcast.5), custom_call_target="tpu_custom_call" | custom-call | tf_op jit(solution)/shard_map/pallas_call | solution.py:203
  2.0 14.9 %all_to_all.20 = f32[8,4,512]{2,1,0:T(4,128)S(1)} all-to-all(f32[8,4,512]{2,1,0:T(4,128)} %get-tuple-element.9), channel_id=1, replica_groups=mesh['y'=8,'core'=2,'grp'=48] {'y'}, dimensions={0} | all-to-all | bytes 131072 | tf_op jit(solution)/shard_map/all_to_all | solution.py:218
  16.9 8.8 %all_gather.6.ghost_ref = f32[16,4,512]{2,1,0:T(4,128)S(1)} all-gather(f32[8,4,512]{2,1,0:T(4,128)S(1)} %all_to_all.20), channel_id=1, replica_groups=mesh['y'=8,'core'=2,'grp'=48] {'core'}, dimensions={0}, use_global_device_ids=true | all-gather | bytes 196608 | tf_op jit(solution)/shard_map/all_gather | solution.py:219
  25.7 0.9 shard_map.87
  26.6 0.0 copy-start.1
  26.6 13.0 %all-to-all-start.1 = ((f32[48,4,128]{2,1,0:T(4,128)}), f32[48,4,128]{2,1,0:T(4,128)S(1)}, u32[]{:S(2)}, u32[]{:S(2)}) async-start(f32[48,4,128]{2,1,0:T(4,128)} %shard_map.87), calls=%async_computation.1 | async-start | bytes 196608 | tf_op jit(solution)/shard_map/all_to_all | solution.py:227
  39.6 0.0 copy-start.3
  39.6 0.0 copy-start.4
  39.6 0.0 copy-done.1
  39.6 0.6 copy-done.3
  40.3 0.0 copy-done.4
  40.3 0.0 copy-start
  40.3 7.7 %shard_map.86.direct_ref = f32[3,512]{1,0:T(4,128)S(1)} custom-call(f32[4,512]{1,0:T(4,128)S(1)} %copy-done.1, f32[16,4,512]{2,1,0:T(4,128)S(1)} %all_gather.6.ghost_ref, s32[2,64]{1,0:T(2,128)S(1)} %copy-done.3, s32[2]{0:T(128)S(1)} %copy-done.4), custom_call_target="tpu_custom_call" | custom-call | flops 671088640 | bytes 200000 | tf_op jit(solution)/shard_map/pallas_call | solution.py:228
  48.0 0.0 copy-start.2
  48.0 3.4 %all-to-all-done.1 = f32[48,4,128]{2,1,0:T(4,128)S(1)} async-done(((f32[48,4,128]{2,1,0:T(4,128)}), f32[48,4,128]{2,1,0:T(4,128)S(1)}, u32[]{:S(2)}, u32[]{:S(2)}) %all-to-all-start.1) | async-done | bytes 98336 | tf_op jit(solution)/shard_map/all_to_all | solution.py:227
  51.5 0.0 copy-done
  51.5 0.0 copy-done.2
  51.5 1.2 %shard_map.88 = (f32[8,4,512]{2,1,0:T(4,128)S(1)}, f32[4,512]{1,0:T(4,128)S(1)}, f32[3,512]{1,0:T(4,128)S(1)}) custom-call(f32[4,512]{1,0:T(4,128)S(1)} %copy-done.1, f32[3,512]{1,0:T(4,128)S(1)} %copy-done, f32[3,512]{1,0:T(4,128)S(1)} %shard_map.86.direct_ref, f32[192,128]{1,0:T(8,128)S(1)} %bitcast.4, s32[2,32]{1,0:T(2,128)S(1)} %copy-done.2), custom_call_target="tpu_custom_call" | custom-call | tf_op jit(solution)/shard_map/pallas_call | solution.py:245
  52.6 9.6 %all_to_all.21 = f32[8,4,512]{2,1,0:T(4,128)S(1)} all-to-all(f32[8,4,512]{2,1,0:T(4,128)S(1)} %get-tuple-element.12), channel_id=1, replica_groups=mesh['y'=8,'core'=2,'grp'=48] {'y'}, dimensions={0} | all-to-all | bytes 131072 | tf_op jit(solution)/shard_map/all_to_all | solution.py:218
  62.2 5.0 %all_gather.7.ghost_ref = f32[16,4,512]{2,1,0:T(4,128)S(1)} all-gather(f32[8,4,512]{2,1,0:T(4,128)S(1)} %all_to_all.21), channel_id=1, replica_groups=mesh['y'=8,'core'=2,'grp'=48] {'core'}, dimensions={0}, use_global_device_ids=true | all-gather | bytes 196608 | tf_op jit(solution)/shard_map/all_gather | solution.py:219
  67.3 0.9 shard_map.90
  68.2 7.7 %all-to-all-start.3 = ((f32[48,4,128]{2,1,0:T(4,128)}), f32[48,4,128]{2,1,0:T(4,128)S(1)}, u32[]{:S(2)}, u32[]{:S(2)}) async-start(f32[48,4,128]{2,1,0:T(4,128)} %shard_map.90), calls=%async_computation.3 | async-start | bytes 196608 | tf_op jit(solution)/shard_map/all_to_all | solution.py:227
  75.9 7.7 %shard_map.89.direct_ref = f32[3,512]{1,0:T(4,128)S(1)} custom-call(f32[4,512]{1,0:T(4,128)S(1)} %get-tuple-element.10.own_ref, f32[16,4,512]{2,1,0:T(4,128)S(1)} %all_gather.7.ghost_ref, s32[2,64]{1,0:T(2,128)S(1)} %copy-done.3, s32[2]{0:T(128)S(1)} %copy-done.4), custom_call_target="tpu_custom_call" | custom-call | flops 671088640 | bytes 200000 | tf_op jit(solution)/shard_map/pallas_call | solution.py:228
  83.6 4.1 %all-to-all-done.3 = f32[48,4,128]{2,1,0:T(4,128)S(1)} async-done(((f32[48,4,128]{2,1,0:T(4,128)}), f32[48,4,128]{2,1,0:T(4,128)S(1)}, u32[]{:S(2)}, u32[]{:S(2)}) %all-to-all-start.3) | async-done | bytes 98336 | tf_op jit(solution)/shard_map/all_to_all | solution.py:227
  87.7 1.8 %shard_map.91 = (f32[3,512]{1,0:T(4,128)}, f32[3,512]{1,0:T(4,128)}, f32[3,512]{1,0:T(4,128)}) custom-call(f32[4,512]{1,0:T(4,128)S(1)} %get-tuple-element.10.own_ref, f32[3,512]{1,0:T(4,128)S(1)} %get-tuple-element.11.vel_ref, f32[3,512]{1,0:T(4,128)S(1)} %shard_map.89.direct_ref, f32[192,128]{1,0:T(8,128)S(1)} %bitcast.3, s32[2,32]{1,0:T(2,128)S(1)} %copy-done.2), custom_call_target="tpu_custom_call" | custom-call | tf_op jit(solution)/shard_map/pallas_call | solution.py:245
Async XLA Ops:
  26.6 13.0 %copy-start.1 = (f32[4,512]{1,0:T(4,128)S(1)}, f32[4,512]{1,0:T(4,128)}, u32[]{:S(2)}) copy-start(f32[4,512]{1,0:T(4,128)} %get-tuple-element.8.own_ref) | copy-start | bytes 24580
  26.6 24.9 %all-to-all-start.1 = ((f32[48,4,128]{2,1,0:T(4,128)}), f32[48,4,128]{2,1,0:T(4,128)S(1)}, u32[]{:S(2)}, u32[]{:S(2)}) async-start(f32[48,4,128]{2,1,0:T(4,128)} %shard_map.87), calls=%async_computation.1 | async-start | bytes 196608 | tf_op jit(solution)/shard_map/all_to_all | solution.py:227
  39.6 0.7 copy-start.3
  39.6 0.7 copy-start.4
  40.3 11.2 %copy-start = (f32[3,512]{1,0:T(4,128)S(1)}, f32[3,512]{1,0:T(4,128)}, u32[]{:S(2)}) copy-start(f32[3,512]{1,0:T(4,128)} %vel_ref.1) | copy-start | bytes 18436
  48.0 3.5 %copy-start.2 = (s32[2,32]{1,0:T(2,128)S(1)}, s32[2,32]{1,0:T(2,128)}, u32[]{:S(2)}) copy-start(s32[2,32]{1,0:T(2,128)} %far_ref.3) | copy-start | bytes 772
  68.2 19.6 %all-to-all-start.3 = ((f32[48,4,128]{2,1,0:T(4,128)}), f32[48,4,128]{2,1,0:T(4,128)S(1)}, u32[]{:S(2)}, u32[]{:S(2)}) async-start(f32[48,4,128]{2,1,0:T(4,128)} %shard_map.90), calls=%async_computation.3 | async-start | bytes 196608 | tf_op jit(solution)/shard_map/all_to_all | solution.py:227

commit v3 on v2

--- a/solution.py
+++ b/solution.py
@@ -7,7 +7,6 @@
 
 timestep = 0.05
 softening = 0.25
-N_Y = 8
 N_SEC = 16
 N_GRP = 48
 B = 256
@@ -20,7 +19,6 @@
 bf16 = jnp.bfloat16
 VMEM = pl.BlockSpec(memory_space=pltpu.VMEM)
 SMEM = pl.BlockSpec(memory_space=pltpu.SMEM)
-WHOLE = pltpu.CompilerParams(vmem_limit_bytes=62 * 1024 * 1024)
 PARAMS = pltpu.CompilerParams(vmem_limit_bytes=40 * 1024 * 1024)
 
 
@@ -47,7 +45,7 @@
     half = pos_ref[...] + (0.5 * timestep) * vel_ref[...]
     own = jnp.concatenate([half, mass_ref[...]], 0)
     own_ref[...] = own
-    for d in range(N_Y):
+    for d in range(N_SEC):
         send_ref[d] = own
 
 
@@ -109,7 +107,7 @@
         a, b, c = split3(jnp.concatenate([source, square, jnp.ones((1, W), f32), pad], 0))
         source_ref[:, W * d : W * d + W] = jnp.concatenate([a, b, c, a, b, a], 0).astype(bf16)
         terms = jnp.concatenate([mass, source * mass], 0)
-        k = (d % N_Y * 2 + d // N_Y) * 2
+        k = 2 * d
         both = []
         for t in range(2):
             first, second = times_ref[t, k : k + 1, :], times_ref[t, k + 1 : k + 2, :]
@@ -146,9 +144,8 @@
             device = block >> 1
             section = (device * 1366) >> 16
             group = device - section * N_GRP
-            at = (section & 1) * N_Y + (section >> 1)
-            row = group * 4 + (at & 3)
-            shift = (128 - (at >> 2) * 32 - (block & 1) * 16) & 127
+            row = group * 4 + (section & 3)
+            shift = (128 - (section >> 2) * 32 - (block & 1) * 16) & 127
             line = moments_ref[pl.ds(row, 1), :]
             picked_ref[b * FAR + e : b * FAR + e + 1, :] = pltpu.roll(line, shift, 1)
     out = []
@@ -187,7 +184,7 @@
     half = current + (0.5 * timestep) * speed
     own = jnp.concatenate([half, own_ref[3:4, :]], 0)
     next_ref[...] = own
-    for d in range(N_Y):
+    for d in range(N_SEC):
         send_ref[d] = own
 
 
@@ -202,7 +199,7 @@
 def on_device(positions, velocities, masses, near_list, near_count, far_list):
     send, own = pl.pallas_call(
         opening,
-        out_shape=(shape(N_Y, 4, W), shape(4, W)),
+        out_shape=(shape(N_SEC, 4, W), shape(4, W)),
         in_specs=[pl.BlockSpec(memory_space=pl.ANY)] * 3,
         out_specs=(VMEM, VMEM),
         scratch_shapes=[
@@ -211,12 +208,11 @@
             pltpu.VMEM((1, W), f32),
             pltpu.SemaphoreType.DMA((3,)),
         ],
-        compiler_params=WHOLE,
-    )(positions, velocities, masses.reshape(1, W))
+        compiler_params=PARAMS,
+    )(*[pltpu.with_memory_space_constraint(v, pltpu.HBM) for v in (positions, velocities, masses.reshape(1, W))])
     speed = velocities
     for step in range(2):
-        along = lax.all_to_all(send, "y", split_axis=0, concat_axis=0, tiled=True)
-        ghosts = lax.all_gather(along, "core", axis=0, tiled=True)
+        ghosts = lax.all_to_all(send, "sec", split_axis=0, concat_axis=0, tiled=True)
         message = pl.pallas_call(
             group_moments,
             out_shape=shape(N_GRP, 4, 128),
@@ -244,7 +240,7 @@
         last = step == 1
         made = pl.pallas_call(
             last_step if last else first_step,
-            out_shape=(shape(3, W),) * 3 if last else (shape(N_Y, 4, W), shape(4, W), shape(3, W)),
+            out_shape=(shape(3, W),) * 3 if last else (shape(N_SEC, 4, W), shape(4, W), shape(3, W)),
             in_specs=[VMEM, VMEM, VMEM, VMEM, SMEM],
             out_specs=(VMEM,) * 3,
             scratch_shapes=[pltpu.VMEM((2 * FAR, 128), f32)],
@@ -256,12 +252,11 @@
 
 
 def solution(mesh):
-    parts = jax.sharding.Mesh(mesh.devices.reshape(N_Y, 2, N_GRP), ("y", "core", "grp"))
-    every = ("y", "core", "grp")
+    every = ("sec", "grp")
     placed = (P(None, every), P(None, every), P(every), P(every, None), P(every), P(every, None))
     return jax.shard_map(
         on_device,
-        mesh=parts,
+        mesh=mesh,
         in_specs=placed,
         out_specs=(P(None, every),) * 3,
         check_vma=False,

time: 90 us -> 87.7 us (0.974)
  blocking collectives: 38.3 us -> 35.4 us
  waiting for transfers between devices: 7.58 us -> 8.86 us
    all_gather x2 -> x0, blocking collectives: 13.8 us -> none  [on_device(): ghosts = lax.all_gather(along, 'core', axis=0, tiled=True)]
    all_to_all x2, blocking collectives: 24.5 us -> 35.4 us  [on_device(): lax.all_to_all(send, 'sec', split_axis=0, concat_axis=0, tiled=True)]
    all_to_all x2, waiting for transfers between devices: 7.58 us -> 8.86 us  [on_device(): lax.all_to_all(message, 'grp', split_axis=0, concat_axis=0, tiled=True)]
  transfers between devices with their start and end apart: 2 -> 2, of which waited for: 2 -> 2; matrix products, arithmetic and copies ran while one was open for 0% -> 0% of each run, Pallas kernels for 17% -> 18%
where the time goes in v3:
time: 87.7 us; the launch traced here: 87.3 us
  blocking collectives  35.4 us (40%)
  Pallas kernels  20.8 us (24%)
  starting transfers between devices  20.8 us (24%)
  waiting for transfers between devices  8.86 us (10%)
    all_to_all x2, blocking collectives, on_device(): lax.all_to_all(send, 'sec', split_axis=0, concat_axis=0, tiled=True)  35.4 us
    all_to_all x2, starting transfers between devices, on_device(): lax.all_to_all(message, 'grp', split_axis=0, concat_axis=0, tiled=True)  20.8 us
    pallas_call x2, Pallas kernels, on_device(): pl.pallas_call(direct, out_shape=shape(3, W), in_specs=[VMEM, VMEM, VMEM,...  15.5 us
    all_to_all x2, waiting for transfers between devices, on_device(): lax.all_to_all(message, 'grp', split_axis=0, concat_axis=0, tiled=True)  8.86 us
    pallas_call x2, Pallas kernels, on_device(): pl.pallas_call(last_step if last else first_step, out_shape=(shape(3, W),...  2.81 us
    pallas_call x2, Pallas kernels, on_device(): pl.pallas_call(group_moments, out_shape=shape(N_GRP, 4, 128), in_specs=[V...  1.76 us
  transfers between devices with their start and end apart: 2, of which 2 were waited for; matrix products, arithmetic and copies ran while one was open for 0% of the time, Pallas kernels for 18%

profile of v3, /device:TPU:1, one launch (start us, length us, event | category | flops | bytes accessed | tf_op | source)
XLA Modules:
  0.0 87.3 jit_solution(16818130110471923282)
XLA Ops:
  0.6 0.8 shard_map.85
  1.4 22.1 %all_to_all.20.ghost_ref = f32[16,4,512]{2,1,0:T(4,128)S(1)} all-to-all(f32[16,4,512]{2,1,0:T(4,128)S(1)} %get-tuple-element.9), channel_id=1, replica_groups=mesh['sec'=16,'grp'=48] {'sec'}, dimensions={0} | all-to-all | bytes 262144 | tf_op jit(solution)/shard_map/all_to_all | solution.py:215
  23.5 0.9 %shard_map.87 = f32[48,4,128]{2,1,0:T(4,128)} custom-call(f32[16,4,512]{2,1,0:T(4,128)S(1)} %all_to_all.20.ghost_ref), custom_call_target="tpu_custom_call" | custom-call | tf_op jit(solution)/shard_map/pallas_call | solution.py:216
  24.4 13.5 %all-to-all-start.1 = ((f32[48,4,128]{2,1,0:T(4,128)}), f32[48,4,128]{2,1,0:T(4,128)S(1)}, u32[]{:S(2)}, u32[]{:S(2)}) async-start(f32[48,4,128]{2,1,0:T(4,128)} %shard_map.87), calls=%async_computation.1 | async-start | bytes 196608 | tf_op jit(solution)/shard_map/all_to_all | solution.py:223
  37.9 0.0 copy-start.2
  37.9 0.0 copy-start.3
  37.9 0.7 copy-done.2
  38.6 0.0 copy-done.3
  38.6 0.0 copy-start
  38.6 7.7 %shard_map.86.direct_ref = f32[3,512]{1,0:T(4,128)S(1)} custom-call(f32[4,512]{1,0:T(4,128)S(1)} %get-tuple-element.8.own_ref, f32[16,4,512]{2,1,0:T(4,128)S(1)} %all_to_all.20.ghost_ref, s32[2,64]{1,0:T(2,128)S(1)} %copy-done.2, s32[2]{0:T(128)S(1)} %copy-done.3), custom_call_target="tpu_custom_call" | custom-call | flops 671088640 | bytes 200000 | tf_op jit(solution)/shard_map/pallas_call | solution.py:224
  46.3 0.0 copy-start.1
  46.3 4.1 %all-to-all-done.1 = f32[48,4,128]{2,1,0:T(4,128)S(1)} async-done(((f32[48,4,128]{2,1,0:T(4,128)}), f32[48,4,128]{2,1,0:T(4,128)S(1)}, u32[]{:S(2)}, u32[]{:S(2)}) %all-to-all-start.1) | async-done | bytes 98336 | tf_op jit(solution)/shard_map/all_to_all | solution.py:223
  50.4 0.0 copy-done
  50.4 0.0 copy-done.1
  50.4 1.1 %shard_map.88 = (f32[16,4,512]{2,1,0:T(4,128)S(1)}, f32[4,512]{1,0:T(4,128)S(1)}, f32[3,512]{1,0:T(4,128)S(1)}) custom-call(f32[4,512]{1,0:T(4,128)S(1)} %get-tuple-element.8.own_ref, f32[3,512]{1,0:T(4,128)S(1)} %copy-done, f32[3,512]{1,0:T(4,128)S(1)} %shard_map.86.direct_ref, f32[192,128]{1,0:T(8,128)S(1)} %bitcast.4, s32[2,32]{1,0:T(2,128)S(1)} %copy-done.1), custom_call_target="tpu_custom_call" | custom-call | tf_op jit(solution)/shard_map/pallas_call | solution.py:241
  51.5 13.3 %all_to_all.21.ghost_ref = f32[16,4,512]{2,1,0:T(4,128)S(1)} all-to-all(f32[16,4,512]{2,1,0:T(4,128)S(1)} %get-tuple-element.12), channel_id=1, replica_groups=mesh['sec'=16,'grp'=48] {'sec'}, dimensions={0} | all-to-all | bytes 262144 | tf_op jit(solution)/shard_map/all_to_all | solution.py:215
  64.8 0.9 %shard_map.90 = f32[48,4,128]{2,1,0:T(4,128)} custom-call(f32[16,4,512]{2,1,0:T(4,128)S(1)} %all_to_all.21.ghost_ref), custom_call_target="tpu_custom_call" | custom-call | tf_op jit(solution)/shard_map/pallas_call | solution.py:216
  65.7 7.3 %all-to-all-start.3 = ((f32[48,4,128]{2,1,0:T(4,128)}), f32[48,4,128]{2,1,0:T(4,128)S(1)}, u32[]{:S(2)}, u32[]{:S(2)}) async-start(f32[48,4,128]{2,1,0:T(4,128)} %shard_map.90), calls=%async_computation.3 | async-start | bytes 196608 | tf_op jit(solution)/shard_map/all_to_all | solution.py:223
  73.0 7.7 %shard_map.89.direct_ref = f32[3,512]{1,0:T(4,128)S(1)} custom-call(f32[4,512]{1,0:T(4,128)S(1)} %get-tuple-element.10.own_ref, f32[16,4,512]{2,1,0:T(4,128)S(1)} %all_to_all.21.ghost_ref, s32[2,64]{1,0:T(2,128)S(1)} %copy-done.2, s32[2]{0:T(128)S(1)} %copy-done.3), custom_call_target="tpu_custom_call" | custom-call | flops 671088640 | bytes 200000 | tf_op jit(solution)/shard_map/pallas_call | solution.py:224
  80.8 4.8 %all-to-all-done.3 = f32[48,4,128]{2,1,0:T(4,128)S(1)} async-done(((f32[48,4,128]{2,1,0:T(4,128)}), f32[48,4,128]{2,1,0:T(4,128)S(1)}, u32[]{:S(2)}, u32[]{:S(2)}) %all-to-all-start.3) | async-done | bytes 98336 | tf_op jit(solution)/shard_map/all_to_all | solution.py:223
  85.6 1.7 %shard_map.91 = (f32[3,512]{1,0:T(4,128)}, f32[3,512]{1,0:T(4,128)}, f32[3,512]{1,0:T(4,128)}) custom-call(f32[4,512]{1,0:T(4,128)S(1)} %get-tuple-element.10.own_ref, f32[3,512]{1,0:T(4,128)S(1)} %get-tuple-element.11.vel_ref, f32[3,512]{1,0:T(4,128)S(1)} %shard_map.89.direct_ref, f32[192,128]{1,0:T(8,128)S(1)} %bitcast.3, s32[2,32]{1,0:T(2,128)S(1)} %copy-done.1), custom_call_target="tpu_custom_call" | custom-call | tf_op jit(solution)/shard_map/pallas_call | solution.py:241
Async XLA Ops:
  24.4 26.0 %all-to-all-start.1 = ((f32[48,4,128]{2,1,0:T(4,128)}), f32[48,4,128]{2,1,0:T(4,128)S(1)}, u32[]{:S(2)}, u32[]{:S(2)}) async-start(f32[48,4,128]{2,1,0:T(4,128)} %shard_map.87), calls=%async_computation.1 | async-start | bytes 196608 | tf_op jit(solution)/shard_map/all_to_all | solution.py:223
  37.9 0.7 copy-start.2
  37.9 0.7 copy-start.3
  38.6 11.8 %copy-start = (f32[3,512]{1,0:T(4,128)S(1)}, f32[3,512]{1,0:T(4,128)}, u32[]{:S(2)}) copy-start(f32[3,512]{1,0:T(4,128)} %vel_ref.1) | copy-start | bytes 18436
  46.3 4.1 %copy-start.1 = (s32[2,32]{1,0:T(2,128)S(1)}, s32[2,32]{1,0:T(2,128)}, u32[]{:S(2)}) copy-start(s32[2,32]{1,0:T(2,128)} %far_ref.3) | copy-start | bytes 772
  65.7 19.9 %all-to-all-start.3 = ((f32[48,4,128]{2,1,0:T(4,128)}), f32[48,4,128]{2,1,0:T(4,128)S(1)}, u32[]{:S(2)}, u32[]{:S(2)}) async-start(f32[48,4,128]{2,1,0:T(4,128)} %shard_map.90), calls=%async_computation.3 | async-start | bytes 196608 | tf_op jit(solution)/shard_map/all_to_all | solution.py:223

commit v4 on v3

v4 whole, which is shorter than its diff:
```python
import jax
import jax.numpy as jnp
from jax import lax
from jax.experimental import pallas as pl
from jax.experimental.pallas import tpu as pltpu
from jax.sharding import PartitionSpec as P

timestep = 0.05
softening = 0.25
N_SEC = 16
N_GRP = 48
B = 256
W = 2 * B
KBLK = 2 * N_SEC
LIST = 64
FAR = 32
CHUNK = 1024
LINE = 4 * W + 128
f32 = jnp.float32
bf16 = jnp.bfloat16
VMEM = pl.BlockSpec(memory_space=pltpu.VMEM)
SMEM = pl.BlockSpec(memory_space=pltpu.SMEM)
PARAMS = pltpu.CompilerParams(vmem_limit_bytes=40 * 1024 * 1024)


def shape(*dims):
    return jax.ShapeDtypeStruct(dims, f32)


def split3(value):
    first = value.astype(bf16).astype(f32)
    rest = value - first
    second = rest.astype(bf16).astype(f32)
    return first, second, rest - second


def opening(pos_hbm, vel_hbm, mass_hbm, far_ref, send_ref, own_ref, pos_ref, vel_ref, mass_ref, lists_ref, sems):
    copies = [
        pltpu.make_async_copy(source, target, sems.at[i])
        for i, (source, target) in enumerate(((pos_hbm, pos_ref), (vel_hbm, vel_ref), (mass_hbm, mass_ref)))
    ]
    for copy in copies:
        copy.start()
    lists_ref[...] = jnp.zeros_like(lists_ref)
    lists_ref[0:2, 0:FAR] = far_ref[...].astype(f32)
    lists = lists_ref[0:1, :] + pltpu.roll(lists_ref[1:2, :], FAR, 1)
    for copy in copies:
        copy.wait()
    half = pos_ref[...] + (0.5 * timestep) * vel_ref[...]
    own_ref[...] = jnp.concatenate([half, mass_ref[...]], 0)
    line = jnp.concatenate([half[0:1], half[1:2], half[2:3], mass_ref[...], lists], 1)
    for d in range(N_SEC):
        send_ref[d] = line


def moments_message(whole):
    section = lax.broadcasted_iota(jnp.int32, (N_SEC, 128), 0)
    lane = lax.broadcasted_iota(jnp.int32, (N_SEC, 128), 1)
    base = section // 4 * 32
    packed = jnp.zeros((N_SEC, 128), f32)

    def total(v):
        return jnp.sum(v, axis=1, keepdims=True)

    for place in range(2):
        x, y, z, m = [w[:, B * place : B * place + B] for w in whole]
        mass = total(m)
        centre = [total(m * v) / mass for v in (x, y, z)]
        dx, dy, dz = [v - c for v, c in zip((x, y, z), centre)]
        radius = dx * dx + dy * dy + dz * dz
        m3 = 3.0 * m
        numbers = [
            mass,
            *centre,
            total(m * (3.0 * dx * dx - radius)),
            total(m * (3.0 * dy * dy - radius)),
            total(m * (3.0 * dz * dz - radius)),
            total(m3 * dx * dy),
            total(m3 * dx * dz),
            total(m3 * dy * dz),
        ]
        for c, number in enumerate(numbers):
            packed = jnp.where(lane == base + (16 * place + c), number, packed)
    return packed[0:4] + packed[4:8] + packed[8:12] + packed[12:16]


def group_moments(ghost_ref, out_ref):
    message = moments_message([ghost_ref[:, 0, W * c : W * c + W] for c in range(4)])
    for k in range(N_GRP):
        out_ref[k] = message


def direct(own_ref, near_ref, count_ref, fetch, source_ref, weight_ref, total_ref, times_ref):
    block = lax.broadcasted_iota(jnp.int32, (KBLK, LIST), 0)
    slot = lax.broadcasted_iota(jnp.int32, (KBLK, LIST), 1)
    for b in range(2):
        hit = (near_ref[b : b + 1, :] == block) & (slot < count_ref[b])
        times = jnp.sum(jnp.where(hit, 1.0, 0.0).astype(f32), axis=1, keepdims=True)
        times_ref[b] = jnp.broadcast_to(times, (KBLK, 128))
    middle = jnp.sum(own_ref[0:3, :], axis=1, keepdims=True) * (1.0 / W)
    target = own_ref[0:3, :] - middle
    norm = jnp.sum(target * target, axis=0, keepdims=True) + softening
    pad = jnp.zeros((3, W), f32)
    a, b, c = split3(jnp.concatenate([-2.0 * target, jnp.ones((1, W), f32), norm, pad], 0))
    targets = jnp.concatenate([a, a, a, b, b, c], 0).astype(bf16)
    for d in range(N_SEC):
        ghost = fetch(d)
        source = ghost[0:3] - middle
        mass = ghost[3:4]
        square = jnp.sum(source * source, axis=0, keepdims=True)
        a, b, c = split3(jnp.concatenate([source, square, jnp.ones((1, W), f32), pad], 0))
        source_ref[:, W * d : W * d + W] = jnp.concatenate([a, b, c, a, b, a], 0).astype(bf16)
        terms = jnp.concatenate([mass, source * mass], 0)
        k = 2 * d
        both = []
        for t in range(2):
            first, second = times_ref[t, k : k + 1, :], times_ref[t, k + 1 : k + 2, :]
            both.append(terms * jnp.concatenate([first, first, second, second], 1))
        a, b, c = split3(jnp.concatenate(both, 0))
        weight_ref[:, W * d : W * d + W] = jnp.concatenate([a, b, c, jnp.zeros_like(a)], 0).astype(bf16)
    total_ref[...] = jnp.zeros_like(total_ref)

    @pl.loop(0, N_SEC * W // CHUNK, unroll=2)
    def _(step):
        at = pl.ds(pl.multiple_of(step * CHUNK, CHUNK), CHUNK)
        square = lax.dot_general(
            source_ref[:, at], targets, (((0,), (0,)), ((), ())), preferred_element_type=f32
        )
        inverse = lax.rsqrt(square)
        cube = inverse * inverse * inverse
        high = cube.astype(bf16)
        low = (cube - high.astype(f32)).astype(bf16)
        weight = weight_ref[:, at]
        total_ref[...] += jnp.dot(weight, high, preferred_element_type=f32) + jnp.dot(
            weight, low, preferred_element_type=f32
        )

    sums = total_ref[0:8] + total_ref[8:16] + total_ref[16:24]
    lane = lax.broadcasted_iota(jnp.int32, (4, W), 1)
    sums = jnp.where(lane < B, sums[0:4], sums[4:8])
    return sums[1:4] - target * sums[0:1]


def first_direct(own_ref, ghost_ref, near_ref, count_ref, vel_ref, out_ref, send_ref, *scratch):
    def fetch(d):
        return jnp.concatenate([ghost_ref[d, :, W * c : W * c + W] for c in range(4)], 0)

    near = direct(own_ref, near_ref, count_ref, fetch, *scratch)
    out_ref[...] = near
    start = own_ref[0:3, :] + timestep * (vel_ref[...] + timestep * near)
    line = jnp.concatenate([start[0:1], start[1:2], start[2:3]], 1)
    for d in range(N_SEC):
        send_ref[d] = line


def last_direct(own_ref, ghost_ref, half_ref, near_ref, count_ref, out_ref, *scratch):
    def fetch(d):
        rows = [half_ref[c, d : d + 1, :] for c in range(3)]
        return jnp.concatenate([*rows, ghost_ref[d, :, 3 * W : 4 * W]], 0)

    out_ref[...] = direct(own_ref, near_ref, count_ref, fetch, *scratch)


def place_of(block):
    device = block >> 1
    section = (device * 1366) >> 16
    group = device - section * N_GRP
    return group * 4 + (section & 3), (section >> 2) * 2 + (block & 1)


def far_sum(x, y, z, picked):
    mass, cx, cy, cz, qxx, qyy, qzz, qxy, qxz, qyz = [picked[:, c : c + 1] for c in range(10)]
    x, y, z = x - cx, y - cy, z - cz
    square = x * x + y * y + z * z + softening
    inverse = lax.rsqrt(square)
    two = inverse * inverse
    five = two * two * inverse
    quad_x = qxx * x + qxy * y + qxz * z
    quad_y = qxy * x + qyy * y + qyz * z
    quad_z = qxz * x + qyz * y + qzz * z
    along = 2.5 * (x * quad_x + y * quad_y + z * quad_z) * two - mass * square
    return [
        jnp.sum((along * r - quad) * five, axis=0, keepdims=True)
        for r, quad in ((x, quad_x), (y, quad_y), (z, quad_z))
    ]


def group_far(ghost_ref, moments_ref, out_ref, hot_ref):
    entries = ghost_ref[:, 0, 4 * W : LINE].astype(jnp.int32)
    row, which = place_of(entries)
    rows = N_GRP * 4
    number = lax.broadcasted_iota(jnp.int32, (rows, 128), 0)
    for d in range(N_SEC):
        hot_ref[:, 128 * d : 128 * d + 128] = jnp.where(number == row[d : d + 1, :], 1.0, 0.0).astype(bf16)
    hot = hot_ref[...]
    picked = sum(
        lax.dot_general(part.astype(bf16), hot, (((0,), (0,)), ((), ())), preferred_element_type=f32)
        for part in split3(moments_ref[...])
    )
    for d in range(N_SEC):
        lines = picked[:, 128 * d : 128 * d + 128]
        mine = lines[0:16]
        for k in range(1, 8):
            mine = jnp.where(which[d : d + 1, :] == k, lines[16 * k : 16 * k + 16], mine)
        mine = mine.T
        for place in range(2):
            at = B * place
            x, y, z = [ghost_ref[d, :, W * c + at : W * c + at + B] for c in range(3)]
            parts = far_sum(x, y, z, mine[FAR * place : FAR * place + FAR])
            for c in range(3):
                out_ref[c, d : d + 1, at : at + B] = parts[c]


def second_moments(start_ref, far_ref, ghost_ref, vel_ref, near_ref, own_ref, out_ref, half_ref, next_ref, speed_ref):
    whole = []
    for c in range(3):
        half = start_ref[:, 0, W * c : W * c + W] + (timestep * timestep) * far_ref[c]
        half_ref[c] = half
        whole.append(half)
    message = moments_message([*whole, ghost_ref[:, 0, 3 * W : 4 * W]])
    for k in range(N_GRP):
        out_ref[k] = message
    section = lax.axis_index("sec")
    far = jnp.concatenate([far_ref[c, pl.ds(section, 1), :] for c in range(3)], 0)
    speed = vel_ref[...] + timestep * (near_ref[...] + far)
    speed_ref[...] = speed
    next_ref[...] = jnp.concatenate([own_ref[0:3, :] + timestep * speed, own_ref[3:4, :]], 0)


def last_step(own_ref, vel_ref, direct_ref, moments_ref, far_ref, pos_ref, speed_ref, accel_ref, picked_ref):
    for b in range(2):
        for e in range(FAR):
            row, which = place_of(far_ref[b, e])
            line = moments_ref[pl.ds(row, 1), :]
            picked_ref[b * FAR + e : b * FAR + e + 1, :] = pltpu.roll(line, (128 - which * 16) & 127, 1)
    far = []
    for b in range(2):
        x, y, z = [own_ref[c : c + 1, B * b : B * b + B] for c in range(3)]
        far.append(jnp.concatenate(far_sum(x, y, z, picked_ref[FAR * b : FAR * b + FAR, :]), 0))
    accel = direct_ref[...] + jnp.concatenate(far, 1)
    accel_ref[...] = accel
    speed = vel_ref[...] + timestep * accel
    speed_ref[...] = speed
    pos_ref[...] = own_ref[0:3, :] + (0.5 * timestep) * speed


def exchange(value, axis):
    return lax.all_to_all(value, axis, split_axis=0, concat_axis=0, tiled=True)


def on_device(positions, velocities, masses, near_list, near_count, far_list):
    message = shape(N_GRP, 4, 128)
    direct_scratch = [
        pltpu.VMEM((48, N_SEC * W), bf16),
        pltpu.VMEM((32, N_SEC * W), bf16),
        pltpu.VMEM((32, W), f32),
        pltpu.VMEM((2, KBLK, 128), f32),
    ]
    pairs = W * N_SEC * W
    direct_cost = pl.CostEstimate(flops=160 * pairs, bytes_accessed=200000, transcendentals=pairs)
    inputs = [pltpu.with_memory_space_constraint(v, pltpu.HBM) for v in (positions, velocities, masses.reshape(1, W))]
    send, own = pl.pallas_call(
        opening,
        out_shape=(shape(N_SEC, 1, LINE), shape(4, W)),
        in_specs=[pl.BlockSpec(memory_space=pl.ANY)] * 3 + [VMEM],
        out_specs=(VMEM, VMEM),
        scratch_shapes=[
            pltpu.VMEM((3, W), f32),
            pltpu.VMEM((3, W), f32),
            pltpu.VMEM((1, W), f32),
            pltpu.VMEM((8, 128), f32),
            pltpu.SemaphoreType.DMA((3,)),
        ],
        compiler_params=PARAMS,
    )(*inputs, far_list)
    ghosts = exchange(send, "sec")
    first = pl.pallas_call(
        group_moments,
        out_shape=message,
        in_specs=[VMEM],
        out_specs=VMEM,
        compiler_params=PARAMS,
    )(ghosts)
    moments = exchange(first, "grp").reshape(N_GRP * 4, 128)
    near, send = pl.pallas_call(
        first_direct,
        out_shape=(shape(3, W), shape(N_SEC, 1, 3 * W)),
        in_specs=[VMEM, VMEM, VMEM, SMEM, VMEM],
        out_specs=(VMEM, VMEM),
        scratch_shapes=direct_scratch,
        compiler_params=PARAMS,
        cost_estimate=direct_cost,
    )(own, ghosts, near_list, near_count, velocities)
    starts = exchange(send, "sec")
    far = pl.pallas_call(
        group_far,
        out_shape=shape(3, N_SEC, W),
        in_specs=[VMEM, VMEM],
        out_specs=VMEM,
        scratch_shapes=[pltpu.VMEM((N_GRP * 4, N_SEC * 128), bf16)],
        compiler_params=PARAMS,
        cost_estimate=pl.CostEstimate(flops=10**10, bytes_accessed=200000, transcendentals=10**6),
    )(ghosts, moments)
    second, halves, own, speed = pl.pallas_call(
        second_moments,
        out_shape=(message, shape(3, N_SEC, W), shape(4, W), shape(3, W)),
        in_specs=[VMEM] * 6,
        out_specs=(VMEM,) * 4,
        compiler_params=PARAMS,
    )(starts, far, ghosts, velocities, near, own)
    moments = exchange(second, "grp").reshape(N_GRP * 4, 128)
    near = pl.pallas_call(
        last_direct,
        out_shape=shape(3, W),
        in_specs=[VMEM, VMEM, VMEM, VMEM, SMEM],
        out_specs=VMEM,
        scratch_shapes=direct_scratch,
        compiler_params=PARAMS,
        cost_estimate=direct_cost,
    )(own, ghosts, halves, near_list, near_count)
    return pl.pallas_call(
        last_step,
        out_shape=(shape(3, W),) * 3,
        in_specs=[VMEM, VMEM, VMEM, VMEM, SMEM],
        out_specs=(VMEM,) * 3,
        scratch_shapes=[pltpu.VMEM((2 * FAR, 128), f32)],
        compiler_params=PARAMS,
    )(own, speed, near, moments, far_list)


def solution(mesh):
    every = ("sec", "grp")
    placed = (P(None, every), P(None, every), P(every), P(every, None), P(every), P(every, None))
    return jax.shard_map(
        on_device,
        mesh=mesh,
        in_specs=placed,
        out_specs=(P(None, every),) * 3,
        check_vma=False,
    )
```

time: 87.7 us -> 87.2 us (level)
  blocking collectives: 35.4 us -> 22.3 us
  starting transfers between devices: 20.8 us -> 25.6 us
  waiting for transfers between devices: 8.86 us -> 12.8 us
  Pallas kernels: 20.8 us -> 24.1 us
    all_to_all x2 -> x1, blocking collectives: 35.4 us -> 22.3 us  [exchange(): return lax.all_to_all(value, axis, split_axis=0, concat_axis=0, tiled=True)]
    all_to_all x2 -> x3, starting transfers between devices: 20.8 us -> 25.6 us  [exchange(): return lax.all_to_all(value, axis, split_axis=0, concat_axis=0, tiled=True)]
    all_to_all x2 -> x3, waiting for transfers between devices: 8.86 us -> 12.8 us  [exchange(): return lax.all_to_all(value, axis, split_axis=0, concat_axis=0, tiled=True)]
    pallas_call x7, Pallas kernels: 20.8 us -> 24.1 us  [the longest x1 8.42 us: on_device(): pl.pallas_call(first_direct, out_shape=(shape(3, W), shape(N_SEC, 1, 3 *...]
  transfers between devices with their start and end apart: 2 -> 3, of which waited for: 2 -> 3; matrix products, arithmetic and copies ran while one was open for 0% -> 0% of each run, Pallas kernels for 18% -> 23%
where the time goes in v4:
time: 87.2 us; the launch traced here: 86.8 us
  starting transfers between devices  25.6 us (29%)
  Pallas kernels  24.1 us (28%)
  blocking collectives  22.3 us (26%)
  waiting for transfers between devices  12.8 us (15%)
  local copies, waits for them, and re-layouts  1.33 us (2%)
    all_to_all x3, starting transfers between devices, exchange(): return lax.all_to_all(value, axis, split_axis=0, concat_axis=0, tiled=True)  25.6 us
    all_to_all x1, blocking collectives, exchange(): return lax.all_to_all(value, axis, split_axis=0, concat_axis=0, tiled=True)  22.3 us
    all_to_all x3, waiting for transfers between devices, exchange(): return lax.all_to_all(value, axis, split_axis=0, concat_axis=0, tiled=True)  12.8 us
    pallas_call x1, Pallas kernels, on_device(): pl.pallas_call(first_direct, out_shape=(shape(3, W), shape(N_SEC, 1, 3 *...  8.42 us
    pallas_call x1, Pallas kernels, on_device(): pl.pallas_call(last_direct, out_shape=shape(3, W), in_specs=[VMEM, VMEM,...  7.76 us
    pallas_call x1, Pallas kernels, on_device(): pl.pallas_call(group_far, out_shape=shape(3, N_SEC, W), in_specs=[VMEM, V...  3.67 us
  transfers between devices with their start and end apart: 3, of which 3 were waited for; matrix products, arithmetic and copies ran while one was open for 0% of the time, Pallas kernels for 23%

profile of v4, /device:TPU:1, one launch (start us, length us, event | category | flops | bytes accessed | tf_op | source)
XLA Modules:
  0.0 86.8 jit_solution(12304556708034242917)
XLA Ops:
  0.6 0.0 copy-start.1
  0.6 0.7 copy-done.1
  1.3 0.8 shard_map.85
  2.1 22.3 %all_to_all.20.ghost_ref = f32[16,1,2176]{2,1,0:T(1,128)S(1)} all-to-all(f32[16,1,2176]{2,1,0:T(1,128)S(1)} %get-tuple-element.12), channel_id=1, replica_groups=mesh['sec'=16,'grp'=48] {'sec'}, dimensions={0} | all-to-all | bytes 278528 | tf_op jit(solution)/shard_map/all_to_all | solution.py:248
  24.4 0.9 %shard_map.87 = f32[48,4,128]{2,1,0:T(4,128)} custom-call(f32[16,1,2176]{2,1,0:T(1,128)S(1)} %all_to_all.20.ghost_ref), custom_call_target="tpu_custom_call" | custom-call | tf_op jit(solution)/shard_map/pallas_call | solution.py:277
  25.3 0.0 copy-start
  25.3 13.6 %all-to-all-start.2 = ((f32[48,4,128]{2,1,0:T(4,128)}), f32[48,4,128]{2,1,0:T(4,128)S(1)}, u32[]{:S(2)}, u32[]{:S(2)}) async-start(f32[48,4,128]{2,1,0:T(4,128)} %shard_map.87), calls=%async_computation.2 | async-start | bytes 196608 | tf_op jit(solution)/shard_map/all_to_all | solution.py:248
  38.9 0.0 copy-start.2
  38.9 0.0 copy-start.3
  38.9 0.0 copy-done
  38.9 0.6 copy-done.2
  39.6 0.0 copy-done.3
  39.6 8.4 %shard_map.86 = (f32[3,512]{1,0:T(4,128)S(1)}, f32[16,1,1536]{2,1,0:T(1,128)}) custom-call(f32[4,512]{1,0:T(4,128)S(1)} %get-tuple-element.11.own_ref, f32[16,1,2176]{2,1,0:T(1,128)S(1)} %all_to_all.20.ghost_ref, s32[2,64]{1,0:T(2,128)S(1)} %copy-done.2, s32[2]{0:T(128)S(1)} %copy-done.3, f32[3,512]{1,0:T(4,128)S(1)} %copy-done), custom_call_target="tpu_custom_call" | custom-call | flops 671088640 | bytes 200000 | tf_op jit(solution)/shard_map/pallas_call | solution.py:285
  48.0 3.4 %all-to-all-done.2 = f32[48,4,128]{2,1,0:T(4,128)S(1)} async-done(((f32[48,4,128]{2,1,0:T(4,128)}), f32[48,4,128]{2,1,0:T(4,128)S(1)}, u32[]{:S(2)}, u32[]{:S(2)}) %all-to-all-start.2) | async-done | bytes 98336 | tf_op jit(solution)/shard_map/all_to_all | solution.py:248
  51.4 4.9 %all-to-all-start.1 = ((f32[16,1,1536]{2,1,0:T(1,128)}), f32[16,1,1536]{2,1,0:T(1,128)S(1)}, u32[]{:S(2)}, u32[]{:S(2)}) async-start(f32[16,1,1536]{2,1,0:T(1,128)} %get-tuple-element.13), calls=%async_computation.1 | async-start | bytes 196608 | tf_op jit(solution)/shard_map/all_to_all | solution.py:248
  56.3 3.7 %shard_map.88.far_ref = f32[3,16,512]{2,1,0:T(8,128)S(1)} custom-call(f32[16,1,2176]{2,1,0:T(1,128)S(1)} %all_to_all.20.ghost_ref, f32[192,128]{1,0:T(8,128)S(1)} %bitcast.4), custom_call_target="tpu_custom_call" | custom-call | flops 10000000000 | bytes 200000 | tf_op jit(solution)/shard_map/pallas_call | solution.py:295
  60.0 4.8 %all-to-all-done.1.start_ref = f32[16,1,1536]{2,1,0:T(1,128)S(1)} async-done(((f32[16,1,1536]{2,1,0:T(1,128)}), f32[16,1,1536]{2,1,0:T(1,128)S(1)}, u32[]{:S(2)}, u32[]{:S(2)}) %all-to-all-start.1) | async-done | bytes 98336 | tf_op jit(solution)/shard_map/all_to_all | solution.py:248
  64.8 0.9 shard_map.89
  65.7 7.0 %all-to-all-start.3 = ((f32[48,4,128]{2,1,0:T(4,128)}), f32[48,4,128]{2,1,0:T(4,128)S(1)}, u32[]{:S(2)}, u32[]{:S(2)}) async-start(f32[48,4,128]{2,1,0:T(4,128)} %get-tuple-element.18), calls=%async_computation.3 | async-start | bytes 196608 | tf_op jit(solution)/shard_map/all_to_all | solution.py:248
  72.7 7.8 %shard_map.90.direct_ref = f32[3,512]{1,0:T(4,128)S(1)} custom-call(f32[4,512]{1,0:T(4,128)S(1)} %get-tuple-element.15.own_ref, f32[16,1,2176]{2,1,0:T(1,128)S(1)} %all_to_all.20.ghost_ref, f32[3,16,512]{2,1,0:T(8,128)S(1)} %get-tuple-element.17.half_ref, s32[2,64]{1,0:T(2,128)S(1)} %copy-done.2, s32[2]{0:T(128)S(1)} %copy-done.3), custom_call_target="tpu_custom_call" | custom-call | flops 671088640 | bytes 200000 | tf_op jit(solution)/shard_map/pallas_call | solution.py:312
  80.5 4.6 %all-to-all-done.3 = f32[48,4,128]{2,1,0:T(4,128)S(1)} async-done(((f32[48,4,128]{2,1,0:T(4,128)}), f32[48,4,128]{2,1,0:T(4,128)S(1)}, u32[]{:S(2)}, u32[]{:S(2)}) %all-to-all-start.3) | async-done | bytes 98336 | tf_op jit(solution)/shard_map/all_to_all | solution.py:248
  85.1 1.7 %shard_map.91 = (f32[3,512]{1,0:T(4,128)}, f32[3,512]{1,0:T(4,128)}, f32[3,512]{1,0:T(4,128)}) custom-call(f32[4,512]{1,0:T(4,128)S(1)} %get-tuple-element.15.own_ref, f32[3,512]{1,0:T(4,128)S(1)} %get-tuple-element.16.vel_ref, f32[3,512]{1,0:T(4,128)S(1)} %shard_map.90.direct_ref, f32[192,128]{1,0:T(8,128)S(1)} %bitcast.3, s32[2,32]{1,0:T(2,128)S(1)} %copy-done.1), custom_call_target="tpu_custom_call" | custom-call | tf_op jit(solution)/shard_map/pallas_call | solution.py:321
Async XLA Ops:
  0.6 0.7 copy-start.1
  25.3 13.6 %copy-start = (f32[3,512]{1,0:T(4,128)S(1)}, f32[3,512]{1,0:T(4,128)}, u32[]{:S(2)}) copy-start(f32[3,512]{1,0:T(4,128)} %vel_ref.3) | copy-start | bytes 18436
  25.3 26.1 %all-to-all-start.2 = ((f32[48,4,128]{2,1,0:T(4,128)}), f32[48,4,128]{2,1,0:T(4,128)S(1)}, u32[]{:S(2)}, u32[]{:S(2)}) async-start(f32[48,4,128]{2,1,0:T(4,128)} %shard_map.87), calls=%async_computation.2 | async-start | bytes 196608 | tf_op jit(solution)/shard_map/all_to_all | solution.py:248
  38.9 0.7 copy-start.2
  38.9 0.7 copy-start.3
  51.4 13.4 %all-to-all-start.1 = ((f32[16,1,1536]{2,1,0:T(1,128)}), f32[16,1,1536]{2,1,0:T(1,128)S(1)}, u32[]{:S(2)}, u32[]{:S(2)}) async-start(f32[16,1,1536]{2,1,0:T(1,128)} %get-tuple-element.13), calls=%async_computation.1 | async-start | bytes 196608 | tf_op jit(solution)/shard_map/all_to_all | solution.py:248
  65.7 19.4 %all-to-all-start.3 = ((f32[48,4,128]{2,1,0:T(4,128)}), f32[48,4,128]{2,1,0:T(4,128)S(1)}, u32[]{:S(2)}, u32[]{:S(2)}) async-start(f32[48,4,128]{2,1,0:T(4,128)} %get-tuple-element.18), calls=%async_computation.3 | async-start | bytes 196608 | tf_op jit(solution)/shard_map/all_to_all | solution.py:248

commit v5 on v4

--- a/solution.py
+++ b/solution.py
@@ -34,23 +34,37 @@
     return first, second, rest - second
 
 
-def opening(pos_hbm, vel_hbm, mass_hbm, far_ref, send_ref, own_ref, pos_ref, vel_ref, mass_ref, lists_ref, sems):
-    copies = [
-        pltpu.make_async_copy(source, target, sems.at[i])
-        for i, (source, target) in enumerate(((pos_hbm, pos_ref), (vel_hbm, vel_ref), (mass_hbm, mass_ref)))
-    ]
+def opening(
+    pos_hbm, vel_hbm, mass_hbm, far_hbm, near_hbm, count_hbm, send_ref, own_ref, times_ref,
+    pos_ref, vel_ref, mass_ref, far_ref, near_ref, count_ref, lists_ref, sems,
+):
+    pairs = (
+        (pos_hbm, pos_ref),
+        (vel_hbm, vel_ref),
+        (mass_hbm, mass_ref),
+        (far_hbm, far_ref),
+        (near_hbm, near_ref),
+        (count_hbm, count_ref),
+    )
+    copies = [pltpu.make_async_copy(source, target, sems.at[i]) for i, (source, target) in enumerate(pairs)]
     for copy in copies:
         copy.start()
     lists_ref[...] = jnp.zeros_like(lists_ref)
+    for copy in copies:
+        copy.wait()
     lists_ref[0:2, 0:FAR] = far_ref[...].astype(f32)
     lists = lists_ref[0:1, :] + pltpu.roll(lists_ref[1:2, :], FAR, 1)
-    for copy in copies:
-        copy.wait()
     half = pos_ref[...] + (0.5 * timestep) * vel_ref[...]
     own_ref[...] = jnp.concatenate([half, mass_ref[...]], 0)
     line = jnp.concatenate([half[0:1], half[1:2], half[2:3], mass_ref[...], lists], 1)
     for d in range(N_SEC):
         send_ref[d] = line
+    block = lax.broadcasted_iota(jnp.int32, (KBLK, LIST), 0)
+    slot = lax.broadcasted_iota(jnp.int32, (KBLK, LIST), 1)
+    for b in range(2):
+        hit = (near_ref[b : b + 1, :] == block) & (slot < count_ref[b])
+        times = jnp.sum(jnp.where(hit, 1.0, 0.0).astype(f32), axis=1, keepdims=True)
+        times_ref[b] = jnp.broadcast_to(times, (KBLK, 128))
 
 
 def moments_message(whole):
@@ -90,13 +104,7 @@
         out_ref[k] = message
 
 
-def direct(own_ref, near_ref, count_ref, fetch, source_ref, weight_ref, total_ref, times_ref):
-    block = lax.broadcasted_iota(jnp.int32, (KBLK, LIST), 0)
-    slot = lax.broadcasted_iota(jnp.int32, (KBLK, LIST), 1)
-    for b in range(2):
-        hit = (near_ref[b : b + 1, :] == block) & (slot < count_ref[b])
-        times = jnp.sum(jnp.where(hit, 1.0, 0.0).astype(f32), axis=1, keepdims=True)
-        times_ref[b] = jnp.broadcast_to(times, (KBLK, 128))
+def direct(own_ref, times_ref, fetch, source_ref, weight_ref):
     middle = jnp.sum(own_ref[0:3, :], axis=1, keepdims=True) * (1.0 / W)
     target = own_ref[0:3, :] - middle
     norm = jnp.sum(target * target, axis=0, keepdims=True) + softening
@@ -118,34 +126,33 @@
             both.append(terms * jnp.concatenate([first, first, second, second], 1))
         a, b, c = split3(jnp.concatenate(both, 0))
         weight_ref[:, W * d : W * d + W] = jnp.concatenate([a, b, c, jnp.zeros_like(a)], 0).astype(bf16)
-    total_ref[...] = jnp.zeros_like(total_ref)
-
-    @pl.loop(0, N_SEC * W // CHUNK, unroll=2)
-    def _(step):
-        at = pl.ds(pl.multiple_of(step * CHUNK, CHUNK), CHUNK)
+    total = jnp.zeros((32, W), f32)
+    for start in range(0, N_SEC * W, CHUNK):
         square = lax.dot_general(
-            source_ref[:, at], targets, (((0,), (0,)), ((), ())), preferred_element_type=f32
+            source_ref[:, start : start + CHUNK],
+            targets,
+            (((0,), (0,)), ((), ())),
+            preferred_element_type=f32,
         )
         inverse = lax.rsqrt(square)
         cube = inverse * inverse * inverse
         high = cube.astype(bf16)
         low = (cube - high.astype(f32)).astype(bf16)
-        weight = weight_ref[:, at]
-        total_ref[...] += jnp.dot(weight, high, preferred_element_type=f32) + jnp.dot(
-            weight, low, preferred_element_type=f32
+        weight = weight_ref[:, start : start + CHUNK]
+        total = total + jnp.dot(
+            jnp.concatenate([weight, weight], 1), jnp.concatenate([high, low], 0), preferred_element_type=f32
         )
-
-    sums = total_ref[0:8] + total_ref[8:16] + total_ref[16:24]
+    sums = total[0:8] + total[8:16] + total[16:24]
     lane = lax.broadcasted_iota(jnp.int32, (4, W), 1)
     sums = jnp.where(lane < B, sums[0:4], sums[4:8])
     return sums[1:4] - target * sums[0:1]
 
 
-def first_direct(own_ref, ghost_ref, near_ref, count_ref, vel_ref, out_ref, send_ref, *scratch):
+def first_direct(own_ref, ghost_ref, times_ref, vel_ref, out_ref, send_ref, *scratch):
     def fetch(d):
         return jnp.concatenate([ghost_ref[d, :, W * c : W * c + W] for c in range(4)], 0)
 
-    near = direct(own_ref, near_ref, count_ref, fetch, *scratch)
+    near = direct(own_ref, times_ref, fetch, *scratch)
     out_ref[...] = near
     start = own_ref[0:3, :] + timestep * (vel_ref[...] + timestep * near)
     line = jnp.concatenate([start[0:1], start[1:2], start[2:3]], 1)
@@ -153,12 +160,12 @@
         send_ref[d] = line
 
 
-def last_direct(own_ref, ghost_ref, half_ref, near_ref, count_ref, out_ref, *scratch):
+def last_direct(own_ref, ghost_ref, half_ref, times_ref, out_ref, *scratch):
     def fetch(d):
         rows = [half_ref[c, d : d + 1, :] for c in range(3)]
         return jnp.concatenate([*rows, ghost_ref[d, :, 3 * W : 4 * W]], 0)
 
-    out_ref[...] = direct(own_ref, near_ref, count_ref, fetch, *scratch)
+    out_ref[...] = direct(own_ref, times_ref, fetch, *scratch)
 
 
 def place_of(block):
@@ -185,7 +192,7 @@
     ]
 
 
-def group_far(ghost_ref, moments_ref, out_ref, hot_ref):
+def group_far(ghost_ref, moments_ref, far_ref, out_ref, hot_ref):
     entries = ghost_ref[:, 0, 4 * W : LINE].astype(jnp.int32)
     row, which = place_of(entries)
     rows = N_GRP * 4
@@ -253,26 +260,27 @@
     direct_scratch = [
         pltpu.VMEM((48, N_SEC * W), bf16),
         pltpu.VMEM((32, N_SEC * W), bf16),
-        pltpu.VMEM((32, W), f32),
-        pltpu.VMEM((2, KBLK, 128), f32),
     ]
     pairs = W * N_SEC * W
     direct_cost = pl.CostEstimate(flops=160 * pairs, bytes_accessed=200000, transcendentals=pairs)
-    inputs = [pltpu.with_memory_space_constraint(v, pltpu.HBM) for v in (positions, velocities, masses.reshape(1, W))]
-    send, own = pl.pallas_call(
+    inputs = (positions, velocities, masses.reshape(1, W), far_list, near_list, near_count)
+    send, own, times = pl.pallas_call(
         opening,
-        out_shape=(shape(N_SEC, 1, LINE), shape(4, W)),
-        in_specs=[pl.BlockSpec(memory_space=pl.ANY)] * 3 + [VMEM],
-        out_specs=(VMEM, VMEM),
+        out_shape=(shape(N_SEC, 1, LINE), shape(4, W), shape(2, KBLK, 128)),
+        in_specs=[pl.BlockSpec(memory_space=pl.ANY)] * 6,
+        out_specs=(VMEM,) * 3,
         scratch_shapes=[
             pltpu.VMEM((3, W), f32),
             pltpu.VMEM((3, W), f32),
             pltpu.VMEM((1, W), f32),
+            pltpu.VMEM((2, FAR), jnp.int32),
+            pltpu.VMEM((2, LIST), jnp.int32),
+            pltpu.SMEM((2,), jnp.int32),
             pltpu.VMEM((8, 128), f32),
-            pltpu.SemaphoreType.DMA((3,)),
+            pltpu.SemaphoreType.DMA((6,)),
         ],
         compiler_params=PARAMS,
-    )(*inputs, far_list)
+    )(*[pltpu.with_memory_space_constraint(v, pltpu.HBM) for v in inputs])
     ghosts = exchange(send, "sec")
     first = pl.pallas_call(
         group_moments,
@@ -285,22 +293,22 @@
     near, send = pl.pallas_call(
         first_direct,
         out_shape=(shape(3, W), shape(N_SEC, 1, 3 * W)),
-        in_specs=[VMEM, VMEM, VMEM, SMEM, VMEM],
+        in_specs=[VMEM] * 4,
         out_specs=(VMEM, VMEM),
         scratch_shapes=direct_scratch,
         compiler_params=PARAMS,
         cost_estimate=direct_cost,
-    )(own, ghosts, near_list, near_count, velocities)
+    )(own, ghosts, times, velocities)
     starts = exchange(send, "sec")
     far = pl.pallas_call(
         group_far,
         out_shape=shape(3, N_SEC, W),
-        in_specs=[VMEM, VMEM],
+        in_specs=[VMEM, VMEM, SMEM],
         out_specs=VMEM,
         scratch_shapes=[pltpu.VMEM((N_GRP * 4, N_SEC * 128), bf16)],
         compiler_params=PARAMS,
         cost_estimate=pl.CostEstimate(flops=10**10, bytes_accessed=200000, transcendentals=10**6),
-    )(ghosts, moments)
+    )(ghosts, moments, far_list)
     second, halves, own, speed = pl.pallas_call(
         second_moments,
         out_shape=(message, shape(3, N_SEC, W), shape(4, W), shape(3, W)),
@@ -312,12 +320,12 @@
     near = pl.pallas_call(
         last_direct,
         out_shape=shape(3, W),
-        in_specs=[VMEM, VMEM, VMEM, VMEM, SMEM],
+        in_specs=[VMEM] * 4,
         out_specs=VMEM,
         scratch_shapes=direct_scratch,
         compiler_params=PARAMS,
         cost_estimate=direct_cost,
-    )(own, ghosts, halves, near_list, near_count)
+    )(own, ghosts, halves, times)
     return pl.pallas_call(
         last_step,
         out_shape=(shape(3, W),) * 3,

time: 87.2 us -> 84.2 us (0.966)
  Pallas kernels: 24.1 us -> 21 us
  waiting for transfers between devices: 12.8 us -> 15.9 us
  starting transfers between devices: 25.6 us -> 23.2 us
    all_to_all x3, waiting for transfers between devices: 12.8 us -> 15.9 us  [exchange(): return lax.all_to_all(value, axis, split_axis=0, concat_axis=0, tiled=True)]
    all_to_all x3, starting transfers between devices: 25.6 us -> 23.2 us  [exchange(): return lax.all_to_all(value, axis, split_axis=0, concat_axis=0, tiled=True)]
    pallas_call x1, Pallas kernels: 8.42 us -> 6.5 us  [on_device(): pl.pallas_call(first_direct, out_shape=(shape(3, W), shape(N_SEC, 1, 3 *...]
    pallas_call x2, Pallas kernels: 8.52 us -> 6.8 us  [the longest x1 5.85 us: on_device(): pl.pallas_call(last_direct, out_shape=shape(3, W), in_specs=[VMEM] * 4, o...]
  transfers between devices with their start and end apart: 3 -> 3, of which waited for: 3 -> 3; matrix products, arithmetic and copies ran while one was open for 0% -> 0% of each run, Pallas kernels for 23% -> 20%
where the time goes in v5:
time: 84.2 us; the launch traced here: 83.7 us
  starting transfers between devices  23.2 us (28%)
  blocking collectives  22.3 us (26%)
  Pallas kernels  21 us (25%)
  waiting for transfers between devices  15.9 us (19%)
    all_to_all x3, starting transfers between devices, exchange(): return lax.all_to_all(value, axis, split_axis=0, concat_axis=0, tiled=True)  23.2 us
    all_to_all x1, blocking collectives, exchange(): return lax.all_to_all(value, axis, split_axis=0, concat_axis=0, tiled=True)  22.3 us
    all_to_all x3, waiting for transfers between devices, exchange(): return lax.all_to_all(value, axis, split_axis=0, concat_axis=0, tiled=True)  15.9 us
    pallas_call x1, Pallas kernels, on_device(): pl.pallas_call(first_direct, out_shape=(shape(3, W), shape(N_SEC, 1, 3 *...  6.5 us
    pallas_call x1, Pallas kernels, on_device(): pl.pallas_call(last_direct, out_shape=shape(3, W), in_specs=[VMEM] * 4, o...  5.85 us
    pallas_call x1, Pallas kernels, on_device(): pl.pallas_call(group_far, out_shape=shape(3, N_SEC, W), in_specs=[VMEM, V...  4.22 us
    pallas_call x1, Pallas kernels, on_device(): pl.pallas_call(last_step, out_shape=(shape(3, W),) * 3, in_specs=[VMEM, V...  1.7 us
  transfers between devices with their start and end apart: 3, of which 3 were waited for; matrix products, arithmetic and copies ran while one was open for 0% of the time, Pallas kernels for 20%

profile of v5, /device:TPU:1, one launch (start us, length us, event | category | flops | bytes accessed | tf_op | source)
XLA Modules:
  0.0 83.7 jit_solution(9564419226413681034)
XLA Ops:
  0.6 1.0 %shard_map.85 = (f32[16,1,2176]{2,1,0:T(1,128)S(1)}, f32[4,512]{1,0:T(4,128)S(1)}, f32[2,32,128]{2,1,0:T(8,128)S(1)}) custom-call(f32[3,512]{1,0:T(4,128)} %pos_hbm.1, f32[3,512]{1,0:T(4,128)} %vel_ref.3, f32[1,512]{1,0:T(1,128)} %bitcast.5, s32[2,32]{1,0:T(2,128)} %far_ref.3, s32[2,64]{1,0:T(2,128)} %near_hbm.1, s32[2]{0:T(128)} %count_hbm.1), custom_call_target="tpu_custom_call" | custom-call | tf_op jit(solution)/shard_map/pallas_call | solution.py:267
  1.6 22.3 %all_to_all.20.ghost_ref = f32[16,1,2176]{2,1,0:T(1,128)S(1)} all-to-all(f32[16,1,2176]{2,1,0:T(1,128)S(1)} %get-tuple-element.13), channel_id=1, replica_groups=mesh['sec'=16,'grp'=48] {'sec'}, dimensions={0} | all-to-all | bytes 278528 | tf_op jit(solution)/shard_map/all_to_all | solution.py:255
  23.9 0.9 %shard_map.87 = f32[48,4,128]{2,1,0:T(4,128)} custom-call(f32[16,1,2176]{2,1,0:T(1,128)S(1)} %all_to_all.20.ghost_ref), custom_call_target="tpu_custom_call" | custom-call | tf_op jit(solution)/shard_map/pallas_call | solution.py:285
  24.8 0.0 copy-start
  24.8 13.6 %all-to-all-start.2 = ((f32[48,4,128]{2,1,0:T(4,128)}), f32[48,4,128]{2,1,0:T(4,128)S(1)}, u32[]{:S(2)}, u32[]{:S(2)}) async-start(f32[48,4,128]{2,1,0:T(4,128)} %shard_map.87), calls=%async_computation.2 | async-start | bytes 196608 | tf_op jit(solution)/shard_map/all_to_all | solution.py:255
  38.4 0.0 copy-done
  38.4 6.5 %shard_map.86 = (f32[3,512]{1,0:T(4,128)S(1)}, f32[16,1,1536]{2,1,0:T(1,128)}) custom-call(f32[4,512]{1,0:T(4,128)S(1)} %get-tuple-element.12.own_ref, f32[16,1,2176]{2,1,0:T(1,128)S(1)} %all_to_all.20.ghost_ref, f32[2,32,128]{2,1,0:T(8,128)S(1)} %get-tuple-element.14.times_ref, f32[3,512]{1,0:T(4,128)S(1)} %copy-done), custom_call_target="tpu_custom_call" | custom-call | flops 671088640 | bytes 200000 | tf_op jit(solution)/shard_map/pallas_call | solution.py:293
  44.9 6.0 %all-to-all-done.2 = f32[48,4,128]{2,1,0:T(4,128)S(1)} async-done(((f32[48,4,128]{2,1,0:T(4,128)}), f32[48,4,128]{2,1,0:T(4,128)S(1)}, u32[]{:S(2)}, u32[]{:S(2)}) %all-to-all-start.2) | async-done | bytes 98336 | tf_op jit(solution)/shard_map/all_to_all | solution.py:255
  50.9 4.9 %all-to-all-start.1 = ((f32[16,1,1536]{2,1,0:T(1,128)}), f32[16,1,1536]{2,1,0:T(1,128)S(1)}, u32[]{:S(2)}, u32[]{:S(2)}) async-start(f32[16,1,1536]{2,1,0:T(1,128)} %get-tuple-element.15), calls=%async_computation.1 | async-start | bytes 196608 | tf_op jit(solution)/shard_map/all_to_all | solution.py:255
  55.8 0.0 copy-start.1
  55.8 0.7 copy-done.1
  56.5 4.2 %shard_map.88.far_ref = f32[3,16,512]{2,1,0:T(8,128)S(1)} custom-call(f32[16,1,2176]{2,1,0:T(1,128)S(1)} %all_to_all.20.ghost_ref, f32[192,128]{1,0:T(8,128)S(1)} %bitcast.4, s32[2,32]{1,0:T(2,128)S(1)} %copy-done.1), custom_call_target="tpu_custom_call" | custom-call | flops 10000000000 | bytes 200000 | tf_op jit(solution)/shard_map/pallas_call | solution.py:303
  60.7 3.6 %all-to-all-done.1.start_ref = f32[16,1,1536]{2,1,0:T(1,128)S(1)} async-done(((f32[16,1,1536]{2,1,0:T(1,128)}), f32[16,1,1536]{2,1,0:T(1,128)S(1)}, u32[]{:S(2)}, u32[]{:S(2)}) %all-to-all-start.1) | async-done | bytes 98336 | tf_op jit(solution)/shard_map/all_to_all | solution.py:255
  64.3 0.9 %shard_map.89 = (f32[48,4,128]{2,1,0:T(4,128)}, f32[3,16,512]{2,1,0:T(8,128)S(1)}, f32[4,512]{1,0:T(4,128)S(1)}, f32[3,512]{1,0:T(4,128)S(1)}) custom-call(f32[16,1,1536]{2,1,0:T(1,128)S(1)} %all-to-all-done.1.start_ref, f32[3,16,512]{2,1,0:T(8,128)S(1)} %shard_map.88.far_ref, f32[16,1,2176]{2,1,0:T(1,128)S(1)} %all_to_all.20.ghost_ref, ...), custom_call_target="tpu_custom_call" | custom-call | tf_op jit(solution)/shard_map/pallas_call | solution.py:312
  65.2 4.7 %all-to-all-start.3 = ((f32[48,4,128]{2,1,0:T(4,128)}), f32[48,4,128]{2,1,0:T(4,128)S(1)}, u32[]{:S(2)}, u32[]{:S(2)}) async-start(f32[48,4,128]{2,1,0:T(4,128)} %get-tuple-element.20), calls=%async_computation.3 | async-start | bytes 196608 | tf_op jit(solution)/shard_map/all_to_all | solution.py:255
  69.9 5.8 %shard_map.90.direct_ref = f32[3,512]{1,0:T(4,128)S(1)} custom-call(f32[4,512]{1,0:T(4,128)S(1)} %get-tuple-element.17.own_ref, f32[16,1,2176]{2,1,0:T(1,128)S(1)} %all_to_all.20.ghost_ref, f32[3,16,512]{2,1,0:T(8,128)S(1)} %get-tuple-element.19.half_ref, f32[2,32,128]{2,1,0:T(8,128)S(1)} %get-tuple-element.14.times_ref), custom_call_target="tpu_custom_call" | custom-call | flops 671088640 | bytes 200000 | tf_op jit(solution)/shard_map/pallas_call | solution.py:320
  75.8 6.3 %all-to-all-done.3 = f32[48,4,128]{2,1,0:T(4,128)S(1)} async-done(((f32[48,4,128]{2,1,0:T(4,128)}), f32[48,4,128]{2,1,0:T(4,128)S(1)}, u32[]{:S(2)}, u32[]{:S(2)}) %all-to-all-start.3) | async-done | bytes 98336 | tf_op jit(solution)/shard_map/all_to_all | solution.py:255
  82.0 1.7 %shard_map.91 = (f32[3,512]{1,0:T(4,128)}, f32[3,512]{1,0:T(4,128)}, f32[3,512]{1,0:T(4,128)}) custom-call(f32[4,512]{1,0:T(4,128)S(1)} %get-tuple-element.17.own_ref, f32[3,512]{1,0:T(4,128)S(1)} %get-tuple-element.18.vel_ref, f32[3,512]{1,0:T(4,128)S(1)} %shard_map.90.direct_ref, f32[192,128]{1,0:T(8,128)S(1)} %bitcast.3, s32[2,32]{1,0:T(2,128)S(1)} %copy-done.1), custom_call_target="tpu_custom_call" | custom-call | tf_op jit(solution)/shard_map/pallas_call | solution.py:329
Async XLA Ops:
  24.8 13.6 %copy-start = (f32[3,512]{1,0:T(4,128)S(1)}, f32[3,512]{1,0:T(4,128)}, u32[]{:S(2)}) copy-start(f32[3,512]{1,0:T(4,128)} %vel_ref.3) | copy-start | bytes 18436
  24.8 26.1 %all-to-all-start.2 = ((f32[48,4,128]{2,1,0:T(4,128)}), f32[48,4,128]{2,1,0:T(4,128)S(1)}, u32[]{:S(2)}, u32[]{:S(2)}) async-start(f32[48,4,128]{2,1,0:T(4,128)} %shard_map.87), calls=%async_computation.2 | async-start | bytes 196608 | tf_op jit(solution)/shard_map/all_to_all | solution.py:255
  50.9 13.4 %all-to-all-start.1 = ((f32[16,1,1536]{2,1,0:T(1,128)}), f32[16,1,1536]{2,1,0:T(1,128)S(1)}, u32[]{:S(2)}, u32[]{:S(2)}) async-start(f32[16,1,1536]{2,1,0:T(1,128)} %get-tuple-element.15), calls=%async_computation.1 | async-start | bytes 196608 | tf_op jit(solution)/shard_map/all_to_all | solution.py:255
  55.8 0.7 copy-start.1
  65.2 16.8 %all-to-all-start.3 = ((f32[48,4,128]{2,1,0:T(4,128)}), f32[48,4,128]{2,1,0:T(4,128)S(1)}, u32[]{:S(2)}, u32[]{:S(2)}) async-start(f32[48,4,128]{2,1,0:T(4,128)} %get-tuple-element.20), calls=%async_computation.3 | async-start | bytes 196608 | tf_op jit(solution)/shard_map/all_to_all | solution.py:255

commit v6 on v5

--- a/solution.py
+++ b/solution.py
@@ -35,7 +35,7 @@
 
 
 def opening(
-    pos_hbm, vel_hbm, mass_hbm, far_hbm, near_hbm, count_hbm, send_ref, own_ref, times_ref,
+    pos_hbm, vel_hbm, mass_hbm, far_hbm, near_hbm, count_hbm, send_ref, own_ref, times_ref, spots_ref,
     pos_ref, vel_ref, mass_ref, far_ref, near_ref, count_ref, lists_ref, sems,
 ):
     pairs = (
@@ -59,6 +59,9 @@
     line = jnp.concatenate([half[0:1], half[1:2], half[2:3], mass_ref[...], lists], 1)
     for d in range(N_SEC):
         send_ref[d] = line
+    row, which = place_of(far_ref[...])
+    spots_ref[0:2, :] = row
+    spots_ref[2:4, :] = (128 - which * 16) & 127
     block = lax.broadcasted_iota(jnp.int32, (KBLK, LIST), 0)
     slot = lax.broadcasted_iota(jnp.int32, (KBLK, LIST), 1)
     for b in range(2):
@@ -192,7 +195,7 @@
     ]
 
 
-def group_far(ghost_ref, moments_ref, far_ref, out_ref, hot_ref):
+def group_far(ghost_ref, moments_ref, out_ref, hot_ref):
     entries = ghost_ref[:, 0, 4 * W : LINE].astype(jnp.int32)
     row, which = place_of(entries)
     rows = N_GRP * 4
@@ -234,12 +237,11 @@
     next_ref[...] = jnp.concatenate([own_ref[0:3, :] + timestep * speed, own_ref[3:4, :]], 0)
 
 
-def last_step(own_ref, vel_ref, direct_ref, moments_ref, far_ref, pos_ref, speed_ref, accel_ref, picked_ref):
+def last_step(own_ref, vel_ref, direct_ref, moments_ref, spots_ref, pos_ref, speed_ref, accel_ref, picked_ref):
     for b in range(2):
         for e in range(FAR):
-            row, which = place_of(far_ref[b, e])
-            line = moments_ref[pl.ds(row, 1), :]
-            picked_ref[b * FAR + e : b * FAR + e + 1, :] = pltpu.roll(line, (128 - which * 16) & 127, 1)
+            line = moments_ref[pl.ds(spots_ref[b, e], 1), :]
+            picked_ref[b * FAR + e : b * FAR + e + 1, :] = pltpu.roll(line, spots_ref[2 + b, e], 1)
     far = []
     for b in range(2):
         x, y, z = [own_ref[c : c + 1, B * b : B * b + B] for c in range(3)]
@@ -264,11 +266,16 @@
     pairs = W * N_SEC * W
     direct_cost = pl.CostEstimate(flops=160 * pairs, bytes_accessed=200000, transcendentals=pairs)
     inputs = (positions, velocities, masses.reshape(1, W), far_list, near_list, near_count)
-    send, own, times = pl.pallas_call(
+    send, own, times, spots = pl.pallas_call(
         opening,
-        out_shape=(shape(N_SEC, 1, LINE), shape(4, W), shape(2, KBLK, 128)),
+        out_shape=(
+            shape(N_SEC, 1, LINE),
+            shape(4, W),
+            shape(2, KBLK, 128),
+            jax.ShapeDtypeStruct((4, FAR), jnp.int32),
+        ),
         in_specs=[pl.BlockSpec(memory_space=pl.ANY)] * 6,
-        out_specs=(VMEM,) * 3,
+        out_specs=(VMEM,) * 4,
         scratch_shapes=[
             pltpu.VMEM((3, W), f32),
             pltpu.VMEM((3, W), f32),
@@ -303,12 +310,12 @@
     far = pl.pallas_call(
         group_far,
         out_shape=shape(3, N_SEC, W),
-        in_specs=[VMEM, VMEM, SMEM],
+        in_specs=[VMEM, VMEM],
         out_specs=VMEM,
         scratch_shapes=[pltpu.VMEM((N_GRP * 4, N_SEC * 128), bf16)],
         compiler_params=PARAMS,
         cost_estimate=pl.CostEstimate(flops=10**10, bytes_accessed=200000, transcendentals=10**6),
-    )(ghosts, moments, far_list)
+    )(ghosts, moments)
     second, halves, own, speed = pl.pallas_call(
         second_moments,
         out_shape=(message, shape(3, N_SEC, W), shape(4, W), shape(3, W)),
@@ -333,7 +340,7 @@
         out_specs=(VMEM,) * 3,
         scratch_shapes=[pltpu.VMEM((2 * FAR, 128), f32)],
         compiler_params=PARAMS,
-    )(own, speed, near, moments, far_list)
+    )(own, speed, near, moments, spots)
 
 
 def solution(mesh):

time: 84.2 us -> 84 us (level)
  waiting for transfers between devices: 15.9 us -> 17.2 us
    all_to_all x3, waiting for transfers between devices: 15.9 us -> 17.2 us  [exchange(): return lax.all_to_all(value, axis, split_axis=0, concat_axis=0, tiled=True)]
  transfers between devices with their start and end apart: 3 -> 3, of which waited for: 3 -> 3; matrix products, arithmetic and copies ran while one was open for 0% -> 0% of each run, Pallas kernels for 20% -> 19%
where the time goes in v6:
time: 84 us; the launch traced here: 83.6 us
  starting transfers between devices  23.2 us (28%)
  blocking collectives  22.3 us (27%)
  Pallas kernels  20.2 us (24%)
  waiting for transfers between devices  17.2 us (20%)
    all_to_all x3, starting transfers between devices, exchange(): return lax.all_to_all(value, axis, split_axis=0, concat_axis=0, tiled=True)  23.2 us
    all_to_all x1, blocking collectives, exchange(): return lax.all_to_all(value, axis, split_axis=0, concat_axis=0, tiled=True)  22.3 us
    all_to_all x3, waiting for transfers between devices, exchange(): return lax.all_to_all(value, axis, split_axis=0, concat_axis=0, tiled=True)  17.2 us
    pallas_call x1, Pallas kernels, on_device(): pl.pallas_call(first_direct, out_shape=(shape(3, W), shape(N_SEC, 1, 3 *...  6.5 us
    pallas_call x1, Pallas kernels, on_device(): pl.pallas_call(last_direct, out_shape=shape(3, W), in_specs=[VMEM] * 4, o...  5.84 us
    pallas_call x1, Pallas kernels, on_device(): pl.pallas_call(group_far, out_shape=shape(3, N_SEC, W), in_specs=[VMEM, V...  3.67 us
  transfers between devices with their start and end apart: 3, of which 3 were waited for; matrix products, arithmetic and copies ran while one was open for 0% of the time, Pallas kernels for 19%

profile of v6, /device:TPU:1, one launch (start us, length us, event | category | flops | bytes accessed | tf_op | source)
XLA Modules:
  0.0 83.6 jit_solution(8709074351844449267)
XLA Ops:
  0.6 1.0 %shard_map.85 = (f32[16,1,2176]{2,1,0:T(1,128)S(1)}, f32[4,512]{1,0:T(4,128)S(1)}, f32[2,32,128]{2,1,0:T(8,128)S(1)}, s32[4,32]{1,0:T(4,128)S(1)}) custom-call(f32[3,512]{1,0:T(4,128)} %pos_hbm.1, f32[3,512]{1,0:T(4,128)} %vel_ref.3, f32[1,512]{1,0:T(1,128)} %bitcast.5, s32[2,32]{1,0:T(2,128)} %far_hbm.1, s32[2,64]{1,0:T(2,128)} %near_hbm.1, s32[2]{0:T(128)} %count_hbm.1), custom_call_target="tpu_custom_call" | custom-call | tf_op jit(solution)/shard_map/pallas_call | solution.py:269
  1.6 22.3 %all_to_all.20.ghost_ref = f32[16,1,2176]{2,1,0:T(1,128)S(1)} all-to-all(f32[16,1,2176]{2,1,0:T(1,128)S(1)} %get-tuple-element.14), channel_id=1, replica_groups=mesh['sec'=16,'grp'=48] {'sec'}, dimensions={0} | all-to-all | bytes 278528 | tf_op jit(solution)/shard_map/all_to_all | solution.py:257
  23.9 0.9 %shard_map.87 = f32[48,4,128]{2,1,0:T(4,128)} custom-call(f32[16,1,2176]{2,1,0:T(1,128)S(1)} %all_to_all.20.ghost_ref), custom_call_target="tpu_custom_call" | custom-call | tf_op jit(solution)/shard_map/pallas_call | solution.py:292
  24.8 0.0 copy-start
  24.8 13.6 %all-to-all-start.2 = ((f32[48,4,128]{2,1,0:T(4,128)}), f32[48,4,128]{2,1,0:T(4,128)S(1)}, u32[]{:S(2)}, u32[]{:S(2)}) async-start(f32[48,4,128]{2,1,0:T(4,128)} %shard_map.87), calls=%async_computation.2 | async-start | bytes 196608 | tf_op jit(solution)/shard_map/all_to_all | solution.py:257
  38.4 0.0 copy-done
  38.4 6.5 %shard_map.86 = (f32[3,512]{1,0:T(4,128)S(1)}, f32[16,1,1536]{2,1,0:T(1,128)}) custom-call(f32[4,512]{1,0:T(4,128)S(1)} %get-tuple-element.13.own_ref, f32[16,1,2176]{2,1,0:T(1,128)S(1)} %all_to_all.20.ghost_ref, f32[2,32,128]{2,1,0:T(8,128)S(1)} %get-tuple-element.15.times_ref, f32[3,512]{1,0:T(4,128)S(1)} %copy-done), custom_call_target="tpu_custom_call" | custom-call | flops 671088640 | bytes 200000 | tf_op jit(solution)/shard_map/pallas_call | solution.py:300
  44.9 6.0 %all-to-all-done.2 = f32[48,4,128]{2,1,0:T(4,128)S(1)} async-done(((f32[48,4,128]{2,1,0:T(4,128)}), f32[48,4,128]{2,1,0:T(4,128)S(1)}, u32[]{:S(2)}, u32[]{:S(2)}) %all-to-all-start.2) | async-done | bytes 98336 | tf_op jit(solution)/shard_map/all_to_all | solution.py:257
  50.9 4.9 %all-to-all-start.1 = ((f32[16,1,1536]{2,1,0:T(1,128)}), f32[16,1,1536]{2,1,0:T(1,128)S(1)}, u32[]{:S(2)}, u32[]{:S(2)}) async-start(f32[16,1,1536]{2,1,0:T(1,128)} %get-tuple-element.16), calls=%async_computation.1 | async-start | bytes 196608 | tf_op jit(solution)/shard_map/all_to_all | solution.py:257
  55.8 3.7 %shard_map.88.far_ref = f32[3,16,512]{2,1,0:T(8,128)S(1)} custom-call(f32[16,1,2176]{2,1,0:T(1,128)S(1)} %all_to_all.20.ghost_ref, f32[192,128]{1,0:T(8,128)S(1)} %bitcast.4), custom_call_target="tpu_custom_call" | custom-call | flops 10000000000 | bytes 200000 | tf_op jit(solution)/shard_map/pallas_call | solution.py:310
  59.5 4.8 %all-to-all-done.1.start_ref = f32[16,1,1536]{2,1,0:T(1,128)S(1)} async-done(((f32[16,1,1536]{2,1,0:T(1,128)}), f32[16,1,1536]{2,1,0:T(1,128)S(1)}, u32[]{:S(2)}, u32[]{:S(2)}) %all-to-all-start.1) | async-done | bytes 98336 | tf_op jit(solution)/shard_map/all_to_all | solution.py:257
  64.3 0.9 %shard_map.89 = (f32[48,4,128]{2,1,0:T(4,128)}, f32[3,16,512]{2,1,0:T(8,128)S(1)}, f32[4,512]{1,0:T(4,128)S(1)}, f32[3,512]{1,0:T(4,128)S(1)}) custom-call(f32[16,1,1536]{2,1,0:T(1,128)S(1)} %all-to-all-done.1.start_ref, f32[3,16,512]{2,1,0:T(8,128)S(1)} %shard_map.88.far_ref, f32[16,1,2176]{2,1,0:T(1,128)S(1)} %all_to_all.20.ghost_ref, ...), custom_call_target="tpu_custom_call" | custom-call | tf_op jit(solution)/shard_map/pallas_call | solution.py:319
  65.2 4.7 %all-to-all-start.3 = ((f32[48,4,128]{2,1,0:T(4,128)}), f32[48,4,128]{2,1,0:T(4,128)S(1)}, u32[]{:S(2)}, u32[]{:S(2)}) async-start(f32[48,4,128]{2,1,0:T(4,128)} %get-tuple-element.21), calls=%async_computation.3 | async-start | bytes 196608 | tf_op jit(solution)/shard_map/all_to_all | solution.py:257
  69.9 5.8 %shard_map.90.direct_ref = f32[3,512]{1,0:T(4,128)S(1)} custom-call(f32[4,512]{1,0:T(4,128)S(1)} %get-tuple-element.18.own_ref, f32[16,1,2176]{2,1,0:T(1,128)S(1)} %all_to_all.20.ghost_ref, f32[3,16,512]{2,1,0:T(8,128)S(1)} %get-tuple-element.20.half_ref, f32[2,32,128]{2,1,0:T(8,128)S(1)} %get-tuple-element.15.times_ref), custom_call_target="tpu_custom_call" | custom-call | flops 671088640 | bytes 200000 | tf_op jit(solution)/shard_map/pallas_call | solution.py:327
  75.7 6.3 %all-to-all-done.3 = f32[48,4,128]{2,1,0:T(4,128)S(1)} async-done(((f32[48,4,128]{2,1,0:T(4,128)}), f32[48,4,128]{2,1,0:T(4,128)S(1)}, u32[]{:S(2)}, u32[]{:S(2)}) %all-to-all-start.3) | async-done | bytes 98336 | tf_op jit(solution)/shard_map/all_to_all | solution.py:257
  82.0 1.5 %shard_map.91 = (f32[3,512]{1,0:T(4,128)}, f32[3,512]{1,0:T(4,128)}, f32[3,512]{1,0:T(4,128)}) custom-call(f32[4,512]{1,0:T(4,128)S(1)} %get-tuple-element.18.own_ref, f32[3,512]{1,0:T(4,128)S(1)} %get-tuple-element.19.vel_ref, f32[3,512]{1,0:T(4,128)S(1)} %shard_map.90.direct_ref, f32[192,128]{1,0:T(8,128)S(1)} %bitcast.3, ...), custom_call_target="tpu_custom_call" | custom-call | tf_op jit(solution)/shard_map/pallas_call | solution.py:336
Async XLA Ops:
  24.8 13.6 %copy-start = (f32[3,512]{1,0:T(4,128)S(1)}, f32[3,512]{1,0:T(4,128)}, u32[]{:S(2)}) copy-start(f32[3,512]{1,0:T(4,128)} %vel_ref.3) | copy-start | bytes 18436
  24.8 26.1 %all-to-all-start.2 = ((f32[48,4,128]{2,1,0:T(4,128)}), f32[48,4,128]{2,1,0:T(4,128)S(1)}, u32[]{:S(2)}, u32[]{:S(2)}) async-start(f32[48,4,128]{2,1,0:T(4,128)} %shard_map.87), calls=%async_computation.2 | async-start | bytes 196608 | tf_op jit(solution)/shard_map/all_to_all | solution.py:257
  50.9 13.4 %all-to-all-start.1 = ((f32[16,1,1536]{2,1,0:T(1,128)}), f32[16,1,1536]{2,1,0:T(1,128)S(1)}, u32[]{:S(2)}, u32[]{:S(2)}) async-start(f32[16,1,1536]{2,1,0:T(1,128)} %get-tuple-element.16), calls=%async_computation.1 | async-start | bytes 196608 | tf_op jit(solution)/shard_map/all_to_all | solution.py:257
  65.2 16.8 %all-to-all-start.3 = ((f32[48,4,128]{2,1,0:T(4,128)}), f32[48,4,128]{2,1,0:T(4,128)S(1)}, u32[]{:S(2)}, u32[]{:S(2)}) async-start(f32[48,4,128]{2,1,0:T(4,128)} %get-tuple-element.21), calls=%async_computation.3 | async-start | bytes 196608 | tf_op jit(solution)/shard_map/all_to_all | solution.py:257

commit v7 on v6

--- a/solution.py
+++ b/solution.py
@@ -16,6 +16,11 @@
 FAR = 32
 CHUNK = 1024
 LINE = 4 * W + 128
+ORDER = [
+    29, 30, 6, 9, 2, 15, 5, 32, 28, 17, 7, 13, 21, 8, 12, 37,
+    0, 24, 1, 36, 19, 39, 25, 31, 38, 18, 16, 20, 42, 27, 34, 3,
+    14, 43, 26, 41, 4, 33, 44, 46, 47, 22, 10, 11, 45, 40, 23, 35,
+]
 f32 = jnp.float32
 bf16 = jnp.bfloat16
 VMEM = pl.BlockSpec(memory_space=pltpu.VMEM)
@@ -175,7 +180,10 @@
     device = block >> 1
     section = (device * 1366) >> 16
     group = device - section * N_GRP
-    return group * 4 + (section & 3), (section >> 2) * 2 + (block & 1)
+    member = jnp.zeros_like(group)
+    for position, number in enumerate(ORDER):
+        member = jnp.where(group == number, position, member)
+    return member * 4 + (section & 3), (section >> 2) * 2 + (block & 1)
 
 
 def far_sum(x, y, z, picked):
@@ -254,7 +262,8 @@
 
 
 def exchange(value, axis):
-    return lax.all_to_all(value, axis, split_axis=0, concat_axis=0, tiled=True)
+    members = [ORDER] if axis == "grp" else None
+    return lax.all_to_all(value, axis, split_axis=0, concat_axis=0, tiled=True, axis_index_groups=members)
 
 
 def on_device(positions, velocities, masses, near_list, near_count, far_list):

time: 84 us -> 82.1 us (0.977)
  waiting for transfers between devices: 17.2 us -> 4.64 us
  starting transfers between devices: 23.2 us -> 33.6 us
    all_to_all x3, waiting for transfers between devices: 17.2 us -> 4.64 us  [exchange(): lax.all_to_all(value, axis, split_axis=0, concat_axis=0, tiled=True, axis...]
    all_to_all x3, starting transfers between devices: 23.2 us -> 33.6 us  [exchange(): lax.all_to_all(value, axis, split_axis=0, concat_axis=0, tiled=True, axis...]
  transfers between devices with their start and end apart: 3 -> 3, of which waited for: 3 -> 1; matrix products, arithmetic and copies ran while one was open for 0% -> 0% of each run, Pallas kernels for 19% -> 20%
where the time goes in v7:
time: 82.1 us; the launch traced here: 81.7 us
  starting transfers between devices  33.6 us (41%)
  blocking collectives  22.3 us (27%)
  Pallas kernels  20.4 us (25%)
  waiting for transfers between devices  4.64 us (6%)
    all_to_all x3, starting transfers between devices, exchange(): lax.all_to_all(value, axis, split_axis=0, concat_axis=0, tiled=True, axis...  33.6 us
    all_to_all x1, blocking collectives, exchange(): lax.all_to_all(value, axis, split_axis=0, concat_axis=0, tiled=True, axis...  22.3 us
    pallas_call x1, Pallas kernels, on_device(): pl.pallas_call(first_direct, out_shape=(shape(3, W), shape(N_SEC, 1, 3 *...  6.5 us
    pallas_call x1, Pallas kernels, on_device(): pl.pallas_call(last_direct, out_shape=shape(3, W), in_specs=[VMEM] * 4, o...  5.85 us
    all_to_all x3, waiting for transfers between devices, exchange(): lax.all_to_all(value, axis, split_axis=0, concat_axis=0, tiled=True, axis...  4.64 us
    pallas_call x1, Pallas kernels, on_device(): pl.pallas_call(group_far, out_shape=shape(3, N_SEC, W), in_specs=[VMEM, V...  3.87 us
  transfers between devices with their start and end apart: 3, of which 1 were waited for; matrix products, arithmetic and copies ran while one was open for 0% of the time, Pallas kernels for 20%

profile of v7, /device:TPU:1, one launch (start us, length us, event | category | flops | bytes accessed | tf_op | source)
XLA Modules:
  0.0 81.7 jit_solution(15435557679650433051)
XLA Ops:
  0.6 1.0 %shard_map.85 = (f32[16,1,2176]{2,1,0:T(1,128)S(1)}, f32[4,512]{1,0:T(4,128)S(1)}, f32[2,32,128]{2,1,0:T(8,128)S(1)}, s32[4,32]{1,0:T(4,128)S(1)}) custom-call(f32[3,512]{1,0:T(4,128)} %pos_hbm.1, f32[3,512]{1,0:T(4,128)} %vel_ref.3, f32[1,512]{1,0:T(1,128)} %bitcast.5, s32[2,32]{1,0:T(2,128)} %far_hbm.1, s32[2,64]{1,0:T(2,128)} %near_hbm.1, s32[2]{0:T(128)} %count_hbm.1), custom_call_target="tpu_custom_call" | custom-call | tf_op jit(solution)/shard_map/pallas_call | solution.py:278
  1.6 22.3 %all_to_all.20.ghost_ref = f32[16,1,2176]{2,1,0:T(1,128)S(1)} all-to-all(f32[16,1,2176]{2,1,0:T(1,128)S(1)} %get-tuple-element.14), channel_id=1, replica_groups=mesh['sec'=16,'grp'=48] {'sec'}, dimensions={0} | all-to-all | bytes 278528 | tf_op jit(solution)/shard_map/all_to_all | solution.py:266
  23.9 0.9 %shard_map.87 = f32[48,4,128]{2,1,0:T(4,128)} custom-call(f32[16,1,2176]{2,1,0:T(1,128)S(1)} %all_to_all.20.ghost_ref), custom_call_target="tpu_custom_call" | custom-call | tf_op jit(solution)/shard_map/pallas_call | solution.py:301
  24.8 0.0 copy-start
  24.8 18.1 %all-to-all-start.2 = ((f32[48,4,128]{2,1,0:T(4,128)}), f32[48,4,128]{2,1,0:T(4,128)S(1)}, u32[]{:S(2)}, u32[]{:S(2)}) async-start(f32[48,4,128]{2,1,0:T(4,128)} %shard_map.87), calls=%async_computation.2 | async-start | bytes 196608 | tf_op jit(solution)/shard_map/all_to_all | solution.py:266
  42.9 0.0 copy-done
  42.9 6.5 %shard_map.86 = (f32[3,512]{1,0:T(4,128)S(1)}, f32[16,1,1536]{2,1,0:T(1,128)}) custom-call(f32[4,512]{1,0:T(4,128)S(1)} %get-tuple-element.13.own_ref, f32[16,1,2176]{2,1,0:T(1,128)S(1)} %all_to_all.20.ghost_ref, f32[2,32,128]{2,1,0:T(8,128)S(1)} %get-tuple-element.15.times_ref, f32[3,512]{1,0:T(4,128)S(1)} %copy-done), custom_call_target="tpu_custom_call" | custom-call | flops 671088640 | bytes 200000 | tf_op jit(solution)/shard_map/pallas_call | solution.py:309
  49.4 0.0 all-to-all-done.2
  49.4 3.5 %all-to-all-start.1 = ((f32[16,1,1536]{2,1,0:T(1,128)}), f32[16,1,1536]{2,1,0:T(1,128)S(1)}, u32[]{:S(2)}, u32[]{:S(2)}) async-start(f32[16,1,1536]{2,1,0:T(1,128)} %get-tuple-element.16), calls=%async_computation.1 | async-start | bytes 196608 | tf_op jit(solution)/shard_map/all_to_all | solution.py:266
  52.9 3.9 %shard_map.88.far_ref = f32[3,16,512]{2,1,0:T(8,128)S(1)} custom-call(f32[16,1,2176]{2,1,0:T(1,128)S(1)} %all_to_all.20.ghost_ref, f32[192,128]{1,0:T(8,128)S(1)} %bitcast.4), custom_call_target="tpu_custom_call" | custom-call | flops 10000000000 | bytes 200000 | tf_op jit(solution)/shard_map/pallas_call | solution.py:319
  56.8 4.6 %all-to-all-done.1.start_ref = f32[16,1,1536]{2,1,0:T(1,128)S(1)} async-done(((f32[16,1,1536]{2,1,0:T(1,128)}), f32[16,1,1536]{2,1,0:T(1,128)S(1)}, u32[]{:S(2)}, u32[]{:S(2)}) %all-to-all-start.1) | async-done | bytes 98336 | tf_op jit(solution)/shard_map/all_to_all | solution.py:266
  61.5 0.9 %shard_map.89 = (f32[48,4,128]{2,1,0:T(4,128)}, f32[3,16,512]{2,1,0:T(8,128)S(1)}, f32[4,512]{1,0:T(4,128)S(1)}, f32[3,512]{1,0:T(4,128)S(1)}) custom-call(f32[16,1,1536]{2,1,0:T(1,128)S(1)} %all-to-all-done.1.start_ref, f32[3,16,512]{2,1,0:T(8,128)S(1)} %shard_map.88.far_ref, f32[16,1,2176]{2,1,0:T(1,128)S(1)} %all_to_all.20.ghost_ref, ...), custom_call_target="tpu_custom_call" | custom-call | tf_op jit(solution)/shard_map/pallas_call | solution.py:328
  62.3 12.0 %all-to-all-start.3 = ((f32[48,4,128]{2,1,0:T(4,128)}), f32[48,4,128]{2,1,0:T(4,128)S(1)}, u32[]{:S(2)}, u32[]{:S(2)}) async-start(f32[48,4,128]{2,1,0:T(4,128)} %get-tuple-element.21), calls=%async_computation.3 | async-start | bytes 196608 | tf_op jit(solution)/shard_map/all_to_all | solution.py:266
  74.3 5.8 %shard_map.90.direct_ref = f32[3,512]{1,0:T(4,128)S(1)} custom-call(f32[4,512]{1,0:T(4,128)S(1)} %get-tuple-element.18.own_ref, f32[16,1,2176]{2,1,0:T(1,128)S(1)} %all_to_all.20.ghost_ref, f32[3,16,512]{2,1,0:T(8,128)S(1)} %get-tuple-element.20.half_ref, f32[2,32,128]{2,1,0:T(8,128)S(1)} %get-tuple-element.15.times_ref), custom_call_target="tpu_custom_call" | custom-call | flops 671088640 | bytes 200000 | tf_op jit(solution)/shard_map/pallas_call | solution.py:336
  80.1 0.0 all-to-all-done.3
  80.1 1.5 %shard_map.91 = (f32[3,512]{1,0:T(4,128)}, f32[3,512]{1,0:T(4,128)}, f32[3,512]{1,0:T(4,128)}) custom-call(f32[4,512]{1,0:T(4,128)S(1)} %get-tuple-element.18.own_ref, f32[3,512]{1,0:T(4,128)S(1)} %get-tuple-element.19.vel_ref, f32[3,512]{1,0:T(4,128)S(1)} %shard_map.90.direct_ref, f32[192,128]{1,0:T(8,128)S(1)} %bitcast.3, ...), custom_call_target="tpu_custom_call" | custom-call | tf_op jit(solution)/shard_map/pallas_call | solution.py:345
Async XLA Ops:
  24.8 18.1 %copy-start = (f32[3,512]{1,0:T(4,128)S(1)}, f32[3,512]{1,0:T(4,128)}, u32[]{:S(2)}) copy-start(f32[3,512]{1,0:T(4,128)} %vel_ref.3) | copy-start | bytes 18436
  24.8 24.6 %all-to-all-start.2 = ((f32[48,4,128]{2,1,0:T(4,128)}), f32[48,4,128]{2,1,0:T(4,128)S(1)}, u32[]{:S(2)}, u32[]{:S(2)}) async-start(f32[48,4,128]{2,1,0:T(4,128)} %shard_map.87), calls=%async_computation.2 | async-start | bytes 196608 | tf_op jit(solution)/shard_map/all_to_all | solution.py:266
  49.4 12.0 %all-to-all-start.1 = ((f32[16,1,1536]{2,1,0:T(1,128)}), f32[16,1,1536]{2,1,0:T(1,128)S(1)}, u32[]{:S(2)}, u32[]{:S(2)}) async-start(f32[16,1,1536]{2,1,0:T(1,128)} %get-tuple-element.16), calls=%async_computation.1 | async-start | bytes 196608 | tf_op jit(solution)/shard_map/all_to_all | solution.py:266
  62.3 17.8 %all-to-all-start.3 = ((f32[48,4,128]{2,1,0:T(4,128)}), f32[48,4,128]{2,1,0:T(4,128)S(1)}, u32[]{:S(2)}, u32[]{:S(2)}) async-start(f32[48,4,128]{2,1,0:T(4,128)} %get-tuple-element.21), calls=%async_computation.3 | async-start | bytes 196608 | tf_op jit(solution)/shard_map/all_to_all | solution.py:266
